TPU v7x, 32 devices: a whole 2x2x4 slice. The times are simulated.
32 devices in a mesh: seq: 8 (over y, x, core), fsdp: 4 (over z).
Axes of the slice: x: 2, y: 2, z: 4, core: 2. Of those that a mesh axis runs over, the one named last changes fastest.
Arguments:
- query: bfloat16 [4, 1280, 4096], P('fsdp', 'seq'), may hold values from -6 to 6
- key: bfloat16 [4, 1280, 4096], P('fsdp', 'seq'), may hold values from -6 to 6
- value: bfloat16 [4, 1280, 4096], P('fsdp', 'seq'), may hold values from -6 to 6
- stream: bfloat16 [4, 1280, 4096], P('fsdp', 'seq'), may hold values from -6 to 6
- targets: int32 [4, 1280], P('fsdp', 'seq'), may hold values from 0 to 3
- short_filter: float32 [7, 3, 2048], replicated, may hold values from -2 to 2
- med_filter: bfloat16 [128, 128], replicated, may hold values from -0.5 to 0.5
- out_weight: bfloat16 [2048, 2048], P('fsdp'), may hold values from -0.125 to 0.125
- head: float32 [4, 2048], replicated, may hold values from -0.09375 to 0.09375
Outputs:
- query_grad: bfloat16 [4, 1280, 4096], P('fsdp', 'seq')
- key_grad: bfloat16 [4, 1280, 4096], P('fsdp', 'seq')
- value_grad: bfloat16 [4, 1280, 4096], P('fsdp', 'seq')
- out_grad: float32 [2048, 2048], P('fsdp')
All inputs are finite; a program needn't handle non-finite values.
Results may differ from a plain program's by a relative error of at most 0.022.
Values may be sent and summed in bfloat16 or wider, within the bound.
A program may use at most 192 MiB of HBM per device.

v0:
```python
import math

import jax
import jax.numpy as jnp
from jax import lax
from jax.sharding import PartitionSpec as P

loss_scale = 64.0


def padded_2(block, sides, width):
    for axis, dim in sides:
        count = lax.axis_size(axis)
        forward = [(i, i + 1) for i in range(count - 1)]
        backward = [(target, source) for source, target in forward]
        low = lax.ppermute(
            lax.slice_in_dim(block, block.shape[dim] - width, None, axis=dim), axis, forward
        )
        high = lax.ppermute(lax.slice_in_dim(block, 0, width, axis=dim), axis, backward)
        block = jnp.concatenate([low, block, high], axis=dim)
    return block


def shifted(padded, conv_taps):
    out_len = padded.shape[1] - conv_taps.shape[0] + 1
    summed = conv_taps[0] * padded[:, :out_len]
    for offset in range(1, conv_taps.shape[0]):
        summed = summed + conv_taps[offset] * padded[:, offset : offset + out_len]
    return summed


def banded(wide, group_taps, flipped, out_len):
    reach = group_taps.shape[0] - 1
    group_count = group_taps.shape[1]
    gen_count, row_total, channels = wide.shape
    per_group = channels // group_count
    block = math.gcd(out_len, 64)
    block_count = out_len // block
    span = block + reach
    outer = jnp.arange(span, dtype=jnp.int32)[:, None]
    inner = jnp.arange(block, dtype=jnp.int32)[None, :]
    if flipped:
        offsets = inner + reach - outer
    else:
        offsets = outer - inner
    valid = (offsets >= 0) & (offsets <= reach)
    table = group_taps.T
    band = jnp.where(
        valid[None], table[:, jnp.clip(offsets, 0, reach)], jnp.zeros((), jnp.bfloat16)
    )
    grouped = wide.reshape(gen_count, row_total, group_count, per_group).transpose(2, 0, 3, 1)
    windows = jnp.concatenate(
        [
            grouped[:, None, :, :, index * block : index * block + span]
            for index in range(block_count)
        ],
        axis=1,
    )
    windows = windows.reshape(group_count, block_count * gen_count * per_group, span)
    mixed = jnp.einsum("gms,gsi->gmi", windows, band, preferred_element_type=jnp.float32)
    mixed = mixed.reshape(group_count, block_count, gen_count, per_group, block).transpose(
        2, 1, 4, 0, 3
    )
    return mixed.reshape(gen_count, out_len, channels)


def pack_rims(upper_part, lower_part, rim_width):
    return jnp.concatenate([upper_part[:, :rim_width], lower_part[:, -rim_width:]], axis=1)


def split_rims(extended, rim_width):
    return (extended[:, :rim_width], extended[:, -rim_width:])


def per_device(query, key, value, stream, targets, short_filter, med_filter, out_weight, head):
    half_width = query.shape[-1] // 2
    genome_count = query.shape[0]
    local_length = query.shape[1]
    row_count = genome_count * local_length
    short_len = short_filter.shape[0]
    long_len = med_filter.shape[0]
    short_taps = short_filter.reshape(short_len, 3 * half_width)
    short_reach = short_len - 1
    long_reach = long_len - 1
    forward_in = jnp.concatenate(
        [query[..., :half_width], key[..., :half_width], value[..., :half_width]], axis=-1
    )
    reverse_in = jnp.concatenate(
        [query[..., half_width:], key[..., half_width:], value[..., half_width:]], axis=-1
    )
    packed = pack_rims(reverse_in, forward_in, short_reach)
    extended = padded_2(packed, (("seq", 1),), short_reach)
    from_left, from_right = split_rims(extended, short_reach)
    forward_feat = shifted(
        jnp.concatenate([from_left, forward_in], axis=1).astype(jnp.float32), short_taps[::-1]
    )
    reverse_feat = shifted(
        jnp.concatenate([reverse_in, from_right], axis=1).astype(jnp.float32), short_taps
    )
    forward_prod = (
        forward_feat[..., half_width : 2 * half_width] * forward_feat[..., 2 * half_width :]
    ).astype(jnp.bfloat16)
    reverse_prod = (
        reverse_feat[..., half_width : 2 * half_width] * reverse_feat[..., 2 * half_width :]
    ).astype(jnp.bfloat16)
    packed_prod = pack_rims(reverse_prod, forward_prod, long_reach)
    extended_prod = padded_2(packed_prod, (("seq", 1),), long_reach)
    prod_left, prod_right = split_rims(extended_prod, long_reach)
    forward_wide = jnp.concatenate([prod_left, forward_prod], axis=1)
    reverse_wide = jnp.concatenate([reverse_prod, prod_right], axis=1)
    forward_mix = banded(forward_wide, med_filter, True, local_length)
    reverse_mix = banded(reverse_wide, med_filter, False, local_length)
    forward_gate = forward_feat[..., :half_width].astype(jnp.bfloat16)
    reverse_gate = reverse_feat[..., :half_width].astype(jnp.bfloat16)
    gated = jnp.stack(
        [
            (forward_gate.astype(jnp.float32) * forward_mix).astype(jnp.bfloat16),
            (reverse_gate.astype(jnp.float32) * reverse_mix).astype(jnp.bfloat16),
        ]
    )
    gated_rows = gated.reshape(2 * row_count, half_width)
    weight_full = lax.all_gather(out_weight, "fsdp", axis=0, tiled=True)
    branch = jnp.dot(gated_rows, weight_full, preferred_element_type=jnp.float32).reshape(
        2, genome_count, local_length, half_width
    )
    state = stream.astype(jnp.float32) + jnp.concatenate([branch[0], branch[1]], axis=-1)
    flipped = head[::-1]
    logits = jnp.dot(
        state[..., :half_width].reshape(row_count, half_width),
        head.T,
        precision=lax.Precision.HIGHEST,
    ) + jnp.dot(
        state[..., half_width:].reshape(row_count, half_width),
        flipped.T,
        precision=lax.Precision.HIGHEST,
    )
    exponent = jnp.exp(logits)
    softmax_out = exponent / jnp.sum(exponent, axis=1, keepdims=True)
    one_hot = (
        targets.reshape(row_count)[:, None] == jnp.arange(head.shape[0], dtype=jnp.int32)[None, :]
    ).astype(jnp.float32)
    logit_grad = loss_scale * (softmax_out - one_hot)
    state_grad = jnp.stack(
        [
            jnp.dot(logit_grad, head, precision=lax.Precision.HIGHEST),
            jnp.dot(logit_grad, flipped, precision=lax.Precision.HIGHEST),
        ]
    ).astype(jnp.bfloat16)
    grad_rows = state_grad.reshape(2 * row_count, half_width)
    gated_grad = lax.dot_general(
        grad_rows, weight_full, (((1,), (1,)), ((), ())), preferred_element_type=jnp.float32
    ).reshape(2, genome_count, local_length, half_width)
    forward_gate_grad = gated_grad[0] * forward_mix
    reverse_gate_grad = gated_grad[1] * reverse_mix
    forward_mix_grad = (gated_grad[0] * forward_gate.astype(jnp.float32)).astype(jnp.bfloat16)
    reverse_mix_grad = (gated_grad[1] * reverse_gate.astype(jnp.float32)).astype(jnp.bfloat16)
    packed_grad = pack_rims(forward_mix_grad, reverse_mix_grad, long_reach)
    extended_grad = padded_2(packed_grad, (("seq", 1),), long_reach)
    grad_left, grad_right = split_rims(extended_grad, long_reach)
    forward_prod_grad = banded(
        jnp.concatenate([forward_mix_grad, grad_right], axis=1), med_filter, False, local_length
    )
    reverse_prod_grad = banded(
        jnp.concatenate([grad_left, reverse_mix_grad], axis=1), med_filter, True, local_length
    )
    forward_feat_grad = jnp.concatenate(
        [
            forward_gate_grad,
            forward_prod_grad * forward_feat[..., 2 * half_width :],
            forward_prod_grad * forward_feat[..., half_width : 2 * half_width],
        ],
        axis=-1,
    )
    reverse_feat_grad = jnp.concatenate(
        [
            reverse_gate_grad,
            reverse_prod_grad * reverse_feat[..., 2 * half_width :],
            reverse_prod_grad * reverse_feat[..., half_width : 2 * half_width],
        ],
        axis=-1,
    )
    packed_feat = pack_rims(forward_feat_grad, reverse_feat_grad, short_reach)
    extended_feat = padded_2(packed_feat.astype(jnp.bfloat16), (("seq", 1),), short_reach).astype(
        packed_feat.dtype
    )
    feat_left, feat_right = split_rims(extended_feat, short_reach)
    forward_in_grad = shifted(jnp.concatenate([forward_feat_grad, feat_right], axis=1), short_taps)
    reverse_in_grad = shifted(
        jnp.concatenate([feat_left, reverse_feat_grad], axis=1), short_taps[::-1]
    )
    query_grad = jnp.concatenate(
        [forward_in_grad[..., :half_width], reverse_in_grad[..., :half_width]], axis=-1
    ).astype(jnp.bfloat16)
    key_grad = jnp.concatenate(
        [
            forward_in_grad[..., half_width : 2 * half_width],
            reverse_in_grad[..., half_width : 2 * half_width],
        ],
        axis=-1,
    ).astype(jnp.bfloat16)
    value_grad = jnp.concatenate(
        [forward_in_grad[..., 2 * half_width :], reverse_in_grad[..., 2 * half_width :]], axis=-1
    ).astype(jnp.bfloat16)
    grad_shard = lax.psum_scatter(
        lax.dot_general(
            gated_rows, grad_rows, (((0,), (0,)), ((), ())), preferred_element_type=jnp.float32
        ).astype(jnp.bfloat16),
        "fsdp",
        scatter_dimension=0,
        tiled=True,
    )
    summed = lax.psum(grad_shard, "seq").astype(jnp.float32)
    out_grad = summed / loss_scale
    return (query_grad, key_grad, value_grad, out_grad)


def solution(mesh):
    placed = (
        P("fsdp", "seq", None),
        P("fsdp", "seq", None),
        P("fsdp", "seq", None),
        P("fsdp", "seq", None),
        P("fsdp", "seq"),
        P(),
        P(),
        P("fsdp", None),
        P(),
    )
    return jax.shard_map(
        per_device,
        mesh=mesh,
        in_specs=placed,
        out_specs=(
            P("fsdp", "seq", None),
            P("fsdp", "seq", None),
            P("fsdp", "seq", None),
            P("fsdp", None),
        ),
        check_vma=False,
    )
```

profile of v0, /device:TPU:0, one launch (start us, length us, event | category | flops | bytes accessed | tf_op | source)
XLA Modules:
  0.0 416.4 jit_solution(6120845152005289313)
XLA Ops:
  8.0 1.4 fusion.86
  9.4 2.1 fusion.84
  12.2 1.3 collective-permute-start.2
  14.2 3.7 collective-permute-start
  17.8 4.7 %rev.2 = f32[4,2048]{1,0:T(4,128)} reverse(f32[4,2048]{1,0:T(4,128)S(1)} %copy-done.27), dimensions={0} | reverse | bytes 65536 | tf_op jit(solution)/shard_map/rev | solution.py:127
  22.8 15.4 %gather_fusion.1 = bf16[5088,128]{1,0:T(8,128)(2,1)S(1)} fusion(bf16[128,128]{0,1:T(8,128)(2,1)S(1)} %bitcast.200, s32[5120]{0:T(1024)S(1)} %get-tuple-element.39), kind=kCustom, calls=%fused_computation.1 | custom fusion | bytes 2625408 | tf_op jit(solution)/shard_map/gather | solution.py:49
  38.2 3.3 copy.41
  41.5 15.4 %gather_fusion = bf16[5088,128]{1,0:T(8,128)(2,1)S(1)} fusion(bf16[128,128]{0,1:T(8,128)(2,1)S(1)} %bitcast.199, s32[5120]{0:T(1024)S(1)} %get-tuple-element.40), kind=kCustom, calls=%fused_computation | custom fusion | bytes 2625408 | tf_op jit(solution)/shard_map/gather | solution.py:49
  56.9 3.3 copy.35
  60.2 1.8 fusion.87
  62.1 2.1 maximum_convert_fusion.1
  64.2 3.2 fusion.20
  67.7 3.9 collective-permute-start.1
  71.6 1.3 maximum_convert_fusion.2
  73.0 3.2 fusion.14
  78.5 1.5 collective-permute-start.3
  84.1 1.5 fusion.32
  85.6 1.4 copy.36
  87.0 5.6 %copy.61 = f32[1,5,32,128,16]{4,3,2,1,0:T(8,128)} copy(f32[1,5,32,128,16]{3,2,4,0,1:T(8,128)S(1)} %bitcast.228) | data formatting | bytes 2621440 | tf_op jit(solution)/shard_map/reshape | solution.py:64
  92.6 10.4 %reshape.687 = f32[160,2048]{1,0:T(8,128)} reshape(f32[1,5,32,128,16]{4,3,2,1,0:T(8,128)} %copy.61) | data formatting | bytes 2621440 | tf_op jit(solution)/shard_map/reshape | solution.py:64
  103.0 9.5 %reshape.685 = f32[1,160,2048]{2,1,0:T(8,128)S(1)} reshape(f32[1,5,32,128,16]{4,3,2,1,0:T(8,128)} %copy.61) | data formatting | bytes 2621440 | tf_op jit(solution)/shard_map/reshape | solution.py:64
  112.5 2.2 pad_maximum_fusion.8
  114.7 1.8 copy.39
  118.3 1.3 copy-done.9
  119.6 1.5 fusion.28
  121.1 2.1 copy.42
  123.1 6.7 %copy.62 = f32[1,5,32,128,16]{4,3,2,1,0:T(8,128)} copy(f32[1,5,32,128,16]{3,2,4,0,1:T(8,128)} %bitcast.229) | data formatting | bytes 2621440 | tf_op jit(solution)/shard_map/reshape | solution.py:64
  129.9 10.7 %reshape.688 = f32[160,2048]{1,0:T(8,128)} reshape(f32[1,5,32,128,16]{4,3,2,1,0:T(8,128)} %copy.62) | data formatting | bytes 2621440 | tf_op jit(solution)/shard_map/reshape | solution.py:64
  140.6 9.4 %reshape.686 = f32[1,160,2048]{2,1,0:T(8,128)S(1)} reshape(f32[1,5,32,128,16]{4,3,2,1,0:T(8,128)} %copy.62) | data formatting | bytes 2621440 | tf_op jit(solution)/shard_map/reshape | solution.py:64
  150.1 1.5 fusion.67
  151.5 1.5 fusion.66
  153.1 8.9 %all-gather.2.cloned.1.call-done = bf16[2048,2048]{1,0:T(8,128)(2,1)} async-done(((bf16[512,2048]{1,0:T(8,128)(2,1)}), bf16[2048,2048]{1,0:T(8,128)(2,1)}) %all-gather.2.cloned.1.call-update) | async-done | bytes 8388624 | tf_op jit(solution)/shard_map/all_gather | solution.py:122
  162.0 5.3 %fusion.89 = f32[320,2048]{1,0:T(8,128)S(1)} fusion(bf16[320,2048]{1,0:T(8,128)(2,1)S(1)} %bitcast.231, bf16[2048,2048]{1,0:T(8,128)(2,1)} %all-gather.2.cloned.1.call-done), kind=kOutput, calls=%fused_computation.196 | convolution fusion | flops 2684354560 | bytes 12320768 | tf_op jit(solution)/shard_map/dot_general | solution.py:123
  171.2 1.3 convolution_bitcast_fusion
  172.5 1.3 convolution_bitcast_fusion.1
  175.0 6.8 %convolution_convert_fusion = bf16[2048,2048]{1,0:T(8,128)(2,1)} fusion(bf16[320,2048]{1,0:T(8,128)(2,1)S(1)} %bitcast.232, bf16[320,2048]{1,0:T(8,128)(2,1)S(1)} %bitcast.233), kind=kOutput, calls=%fused_computation.2 | convolution fusion | flops 2688548864 | bytes 11010048 | tf_op jit(solution)/shard_map/dot_general | solution.py:205
  181.7 5.9 %fusion.90 = f32[320,2048]{1,0:T(8,128)S(1)} fusion(bf16[320,2048]{1,0:T(8,128)(2,1)} %bitcast.234, bf16[2048,2048]{1,0:T(8,128)(2,1)} %all-gather.2.cloned.1.call-done), kind=kOutput, calls=%fused_computation.197 | convolution fusion | flops 2684354560 | bytes 12320768 | tf_op jit(solution)/shard_map/dot_general | solution.py:150
  187.6 2.0 fusion.35
  191.6 2.8 collective-permute-start.5
  194.4 1.3 collective-permute-start.4
  195.7 3.6 multiply_bitcast_fusion.1
  199.4 2.3 pad_maximum_fusion.10
  201.6 1.9 copy.55
  203.6 2.2 pad_maximum_fusion.9
  205.8 1.8 copy.47
  210.6 2.9 fusion.26
  213.5 3.2 copy.49
  219.7 1.5 fusion.30
  221.2 1.4 copy.57
  222.6 5.6 %copy.69 = f32[1,5,32,128,16]{4,3,2,1,0:T(8,128)} copy(f32[1,5,32,128,16]{3,2,4,0,1:T(8,128)S(1)} %bitcast.230) | data formatting | bytes 2621440 | tf_op jit(solution)/shard_map/reshape | solution.py:64
  228.1 10.3 %reshape.690 = f32[1,160,2048]{2,1,0:T(8,128)} reshape(f32[1,5,32,128,16]{4,3,2,1,0:T(8,128)} %copy.69) | data formatting | bytes 2621440 | tf_op jit(solution)/shard_map/reshape | solution.py:64
  238.5 2.5 slice_multiply_fusion.26
  241.2 1.3 copy-done.20
  242.5 7.4 %collective-permute-start.6 = (bf16[1,6,6144]{2,1,0:T(8,128)(2,1)S(1)}, bf16[1,6,6144]{2,1,0:T(8,128)(2,1)S(1)}, u32[]{:S(2)}, u32[]{:S(2)}) collective-permute-start(bf16[1,6,6144]{2,1,0:T(8,128)(2,1)S(1)} %slice.705), channel_id=1, source_target_pairs={{0,4},{4,8},{8,12},{12,16},{16,20},{20,24},{24,28},{1,5},{5,9},{9,... | collective-permute-start | bytes 221192 | tf_op jit(solution)/shard_map/ppermute | solution.py:16
  249.9 7.0 %copy.67 = f32[1,5,32,128,16]{4,3,2,1,0:T(8,128)} copy(f32[1,5,32,128,16]{3,2,4,0,1:T(8,128)} %bitcast.227) | data formatting | bytes 2621440 | tf_op jit(solution)/shard_map/reshape | solution.py:64
  256.9 10.5 %reshape.689 = f32[1,160,2048]{2,1,0:T(8,128)} reshape(f32[1,5,32,128,16]{4,3,2,1,0:T(8,128)} %copy.67) | data formatting | bytes 2621440 | tf_op jit(solution)/shard_map/reshape | solution.py:64
  267.3 2.5 slice_multiply_fusion.28
  270.1 1.3 collective-permute-start.7
  274.1 3.9 fusion.8
  280.3 3.6 fusion.2
  285.0 55.0 %reduce-scatter.2.cloned.1.call-done = bf16[512,2048]{1,0:T(8,128)(2,1)} async-done(((bf16[2048,2048]{1,0:T(8,128)(2,1)}), bf16[512,2048]{1,0:T(8,128)(2,1)}) %reduce-scatter.2.cloned.1.call-update) | async-done | bytes 2097168 | tf_op jit(solution)/shard_map/reduce_scatter | solution.py:204
  340.1 2.2 pad_maximum_fusion.6
  344.6 60.9 %all-reduce.2.cloned.1.call-done = bf16[512,2048]{1,0:T(8,128)(2,1)} async-done(((bf16[512,2048]{1,0:T(8,128)(2,1)}), bf16[512,2048]{1,0:T(8,128)(2,1)}) %all-reduce.2.cloned.1.call-update) | async-done | bytes 2097168 | tf_op jit(solution)/shard_map/psum | solution.py:212
  405.5 4.2 convert_multiply_fusion
  (136 shorter events, 33.0 us)
Async XLA Ops:
  7.2 15.6 %copy-start = (bf16[128,128]{1,0:T(8,128)(2,1)S(1)}, bf16[128,128]{1,0:T(8,128)(2,1)}, u32[]{:S(2)}) copy-start(bf16[128,128]{1,0:T(8,128)(2,1)} %param.15) | copy-start | bytes 98308
  7.2 154.8 %all-gather.2.cloned.1.call-start = ((), (), s32[]{:S(2)}) async-start(), calls=%async_computation.1 | async-start | bytes 10485760 | tf_op jit(solution)/shard_map/all_gather | solution.py:122
  7.9 332.1 %reduce-scatter.2.cloned.1.call-start = ((), (), s32[]{:S(2)}) async-start(), calls=%async_computation.2 | async-start | bytes 10485760 | tf_op jit(solution)/shard_map/reduce_scatter | solution.py:204
  9.3 4.8 %copy-start.11 = (bf16[1,160,2048]{2,1,0:T(8,128)(2,1)}, bf16[1,160,2048]{2,1,0:T(8,128)(2,1)S(1)}, u32[]{:S(2)}) copy-start(bf16[1,160,2048]{2,1,0:T(8,128)(2,1)S(1)} %get-tuple-element.24) | copy-start | bytes 1966084
  9.3 8.5 %copy-start.27 = (f32[4,2048]{1,0:T(4,128)S(1)}, f32[4,2048]{1,0:T(4,128)}, u32[]{:S(2)}) copy-start(f32[4,2048]{1,0:T(4,128)} %param.17) | copy-start | bytes 98308
  11.5 6.4 %copy-start.12 = (bf16[1,160,2048]{2,1,0:T(8,128)(2,1)}, bf16[1,160,2048]{2,1,0:T(8,128)(2,1)S(1)}, u32[]{:S(2)}) copy-start(bf16[1,160,2048]{2,1,0:T(8,128)(2,1)S(1)} %get-tuple-element.20) | copy-start | bytes 1966084
  11.5 6.3 %copy-start.13 = (bf16[1,160,2048]{2,1,0:T(8,128)(2,1)}, bf16[1,160,2048]{2,1,0:T(8,128)(2,1)S(1)}, u32[]{:S(2)}) copy-start(bf16[1,160,2048]{2,1,0:T(8,128)(2,1)S(1)} %get-tuple-element.38) | copy-start | bytes 1966084
  12.2 59.4 %collective-permute-start.2 = (bf16[1,6,6144]{2,1,0:T(8,128)(2,1)}, bf16[1,6,6144]{2,1,0:T(8,128)(2,1)}, u32[]{:S(2)}, u32[]{:S(2)}) collective-permute-start(bf16[1,6,6144]{2,1,0:T(8,128)(2,1)} %pad_maximum_fusion.13), channel_id=1, source_target_pairs={{4,0},{8,4},{12,8},{16,12},{20,16},{24,20},{28,24},{5,1},{9,5},{13... | collective-permute-start | bytes 221192 | tf_op jit(solution)/shard_map/ppermute | solution.py:19
  14.2 47.9 %collective-permute-start = (bf16[1,6,6144]{2,1,0:T(8,128)(2,1)}, bf16[1,6,6144]{2,1,0:T(8,128)(2,1)}, u32[]{:S(2)}, u32[]{:S(2)}) collective-permute-start(bf16[1,6,6144]{2,1,0:T(8,128)(2,1)} %pad_maximum_fusion.15), channel_id=1, source_target_pairs={{0,4},{4,8},{8,12},{12,16},{16,20},{20,24},{24,28},{1,5},{5,9},{9,... | collective-permute-start | bytes 221192 | tf_op jit(solution)/shard_map/ppermute | solution.py:16
  62.0 10.9 %copy-start.23 = (f32[1,3,2048]{2,0,1:T(1,128)}, f32[1,3,2048]{2,0,1:T(1,128)S(1)}, u32[]{:S(2)}) copy-start(f32[1,3,2048]{2,0,1:T(1,128)S(1)} %get-tuple-element.33) | copy-start | bytes 73732
  62.1 10.9 %copy-start.25 = (f32[1,3,2048]{2,0,1:T(1,128)}, f32[1,3,2048]{2,0,1:T(1,128)S(1)}, u32[]{:S(2)}) copy-start(f32[1,3,2048]{2,0,1:T(1,128)S(1)} %get-tuple-element.34) | copy-start | bytes 73732
  67.4 5.6 %copy-start.2 = (f32[1,160,6144]{2,1,0:T(8,128)}, f32[1,160,6144]{2,1,0:T(8,128)S(1)}, u32[]{:S(2)}) copy-start(f32[1,160,6144]{2,1,0:T(8,128)S(1)} %fusion.20) | copy-start | bytes 11796484
  67.7 12.3 %collective-permute-start.1 = (bf16[1,127,2048]{2,1,0:T(8,128)(2,1)S(1)}, bf16[1,127,2048]{2,1,0:T(8,128)(2,1)S(1)}, u32[]{:S(2)}, u32[]{:S(2)}) collective-permute-start(bf16[1,127,2048]{2,1,0:T(8,128)(2,1)S(1)} %slice.427), channel_id=1, source_target_pairs={{0,4},{4,8},{8,12},{12,16},{16,20},{20,24},{24,28},{1,5},{5,9},{9,... | collective-permute-start | bytes 1560584 | tf_op jit(solution)/shard_map/ppermute | solution.py:16
  76.2 3.8 copy-start.3
  76.4 1.0 copy-start.16
  78.5 34.0 %collective-permute-start.3 = (bf16[1,127,2048]{2,1,0:T(8,128)(2,1)}, bf16[1,127,2048]{2,1,0:T(8,128)(2,1)}, u32[]{:S(2)}, u32[]{:S(2)}) collective-permute-start(bf16[1,127,2048]{2,1,0:T(8,128)(2,1)} %slice.443), channel_id=1, source_target_pairs={{4,0},{8,4},{12,8},{16,12},{20,16},{24,20},{28,24},{5,1},{9,5},{13... | collective-permute-start | bytes 1560584 | tf_op jit(solution)/shard_map/ppermute | solution.py:19
  82.6 1.6 copy-start.7
  103.0 9.6 %copy-start.17 = (bf16[1,160,2048]{2,1,0:T(8,128)(2,1)S(1)}, bf16[1,160,2048]{2,1,0:T(8,128)(2,1)}, u32[]{:S(2)}) copy-start(bf16[1,160,2048]{2,1,0:T(8,128)(2,1)} %copy-done.16) | copy-start | bytes 1966084
  118.0 1.6 copy-start.9
  167.2 1.3 copy-start.22
  167.5 1.3 copy-start.29
  168.5 1.5 copy-start.28
  168.5 2.6 copy-start.30
  173.9 1.1 copy-start.21
  189.7 1.0 copy-start.14
  191.6 7.8 %collective-permute-start.5 = (bf16[1,127,2048]{2,1,0:T(8,128)(2,1)}, bf16[1,127,2048]{2,1,0:T(8,128)(2,1)}, u32[]{:S(2)}, u32[]{:S(2)}) collective-permute-start(bf16[1,127,2048]{2,1,0:T(8,128)(2,1)} %slice.461), channel_id=1, source_target_pairs={{0,4},{4,8},{8,12},{12,16},{16,20},{20,24},{24,28},{1,5},{5,9},{9,... | collective-permute-start | bytes 1560584 | tf_op jit(solution)/shard_map/ppermute | solution.py:16
  194.4 9.2 %collective-permute-start.4 = (bf16[1,127,2048]{2,1,0:T(8,128)(2,1)}, bf16[1,127,2048]{2,1,0:T(8,128)(2,1)}, u32[]{:S(2)}, u32[]{:S(2)}) collective-permute-start(bf16[1,127,2048]{2,1,0:T(8,128)(2,1)} %slice.454), channel_id=1, source_target_pairs={{4,0},{8,4},{12,8},{16,12},{20,16},{24,20},{28,24},{5,1},{9,5},{13... | collective-permute-start | bytes 1560584 | tf_op jit(solution)/shard_map/ppermute | solution.py:19
  195.7 209.8 %all-reduce.2.cloned.1.call-start = ((), (), s32[]{:S(2)}) async-start(), calls=%async_computation.3 | async-start | bytes 4194304 | tf_op jit(solution)/shard_map/psum | solution.py:212
  195.7 3.6 copy-start.15
  209.0 1.6 copy-start.10
  218.1 1.6 copy-start.8
  238.5 2.5 copy-start.4
  241.2 1.3 copy-start.20
  242.5 29.9 %collective-permute-start.6 = (bf16[1,6,6144]{2,1,0:T(8,128)(2,1)S(1)}, bf16[1,6,6144]{2,1,0:T(8,128)(2,1)S(1)}, u32[]{:S(2)}, u32[]{:S(2)}) collective-permute-start(bf16[1,6,6144]{2,1,0:T(8,128)(2,1)S(1)} %slice.705), channel_id=1, source_target_pairs={{0,4},{4,8},{8,12},{12,16},{16,20},{20,24},{24,28},{1,5},{5,9},{9,... | collective-permute-start | bytes 221192 | tf_op jit(solution)/shard_map/ppermute | solution.py:16
  267.3 2.5 copy-start.6
  270.1 3.2 collective-permute-start.7
  273.4 0.7 copy-start.24
  273.4 0.7 copy-start.26
  278.0 1.8 copy-start.5
  284.0 56.1 %copy-start.19 = (bf16[1,160,2048]{2,1,0:T(8,128)(2,1)S(1)}, bf16[1,160,2048]{2,1,0:T(8,128)(2,1)}, u32[]{:S(2)}) copy-start(bf16[1,160,2048]{2,1,0:T(8,128)(2,1)} %get-tuple-element.14) | copy-start | bytes 1966084
  284.0 58.4 %copy-start.18 = (bf16[1,160,2048]{2,1,0:T(8,128)(2,1)S(1)}, bf16[1,160,2048]{2,1,0:T(8,128)(2,1)}, u32[]{:S(2)}) copy-start(bf16[1,160,2048]{2,1,0:T(8,128)(2,1)} %get-tuple-element.15) | copy-start | bytes 1966084
  343.5 66.2 %copy-start.1 = (bf16[128,128]{1,0:T(8,128)(2,1)S(1)}, bf16[128,128]{1,0:T(8,128)(2,1)}, u32[]{:S(2)}) copy-start(bf16[128,128]{1,0:T(8,128)(2,1)} %param.15) | copy-start | bytes 98308
Sparse Core Ops, SparseCore 0:
  9.6 152.3 all-gather.1
  195.8 144.2 reduce-scatter.1
  343.3 62.1 all-reduce.1
where the time goes:
time: 424 us; the launch traced here: 416 us
  local copies, waits for them, and re-layouts  172 us (41%)
  waiting for transfers between devices  126 us (30%)
  other arithmetic  50.3 us (12%)
  matrix products  30.1 us (7%)
  starting transfers between devices  23.1 us (5%)
  between operations  14.8 us (3%)
    reshape x10, local copies, waits for them, and re-layouts, banded(): return mixed.reshape(gen_count, out_len, channels)  85.7 us
    psum x1, waiting for transfers between devices, per_device(): summed = lax.psum(grad_shard, 'seq').astype(jnp.float32)  60.9 us
    reduce_scatter x1, waiting for transfers between devices, per_device(): lax.psum_scatter(lax.dot_general(gated_rows, grad_rows, (((0,), (0,)), ((...  55 us
    gather x4, local copies, waits for them, and re-layouts, banded(): table[:, jnp.clip(offsets, 0, reach)]  37.3 us
    ppermute x4, starting transfers between devices, padded_2(): lax.ppermute(lax.slice_in_dim(block, block.shape[dim] - width, None, axis...  17.7 us
    unnamed x78, local copies, waits for them, and re-layouts  15.8 us
    all_gather x1, waiting for transfers between devices, per_device(): weight_full = lax.all_gather(out_weight, 'fsdp', axis=0, tiled=True)  8.86 us
  transfers between devices with their start and end apart: 11, of which 4 were waited for; matrix products, arithmetic and copies ran while one was open for 50% of the time, Pallas kernels for 0%

commit v1 on v0

v1 whole, which is shorter than its diff:
```python
import jax
import jax.numpy as jnp
from jax import lax
from jax.experimental import pallas as pl
from jax.experimental.pallas import tpu as pltpu
from jax.sharding import PartitionSpec as P

loss_scale = 64.0
LANES = 256
EDGE = 8
BLOCK = 128
VMEM_LIMIT = 48 * 1024 * 1024


def split_bf16(x):
    high = x.astype(jnp.bfloat16)
    low = (x - high.astype(jnp.float32)).astype(jnp.bfloat16)
    return high, low


def mm(a, b, ca=1, cb=0):
    return lax.dot_general(a, b, (((ca,), (cb,)), ((), ())), preferred_element_type=jnp.float32)


def banded(x_ref, base_ref, out_ref, tail_first):
    per_group = LANES // base_ref.shape[1]
    rows = out_ref.shape[0]
    rest = rows - BLOCK
    span = BLOCK + rest
    big_in, small_in = (rest, 0) if tail_first else (0, BLOCK)
    big_out, small_out = (rest, 0) if tail_first else (0, BLOCK)
    lane = lax.broadcasted_iota(jnp.int32, (1, BLOCK), 1) // per_group
    for part in range(LANES // BLOCK):
        cols = slice(part * BLOCK, (part + 1) * BLOCK)
        x_big = x_ref[big_in : big_in + 2 * BLOCK, cols]
        x_small = x_ref[small_in : small_in + span, cols]
        big = small = None
        for index in range(BLOCK // per_group):
            g = part * (BLOCK // per_group) + index
            row = jnp.broadcast_to(base_ref[0, g : g + 1, :], (BLOCK, 2 * BLOCK))
            toeplitz = pltpu.roll(row, 0, 1, stride=1, stride_axis=0).astype(jnp.bfloat16)
            one_big = mm(toeplitz, x_big)
            one_small = mm(toeplitz[:rest, :span], x_small)
            if index == 0:
                big, small = one_big, one_small
            else:
                here = lane == index
                big = jnp.where(here, one_big, big)
                small = jnp.where(here, one_small, small)
        out_ref[big_out : big_out + BLOCK, cols] = big
        out_ref[small_out : small_out + rest, cols] = small


def featured_kernel(q_ref, k_ref, v_ref, rim_ref, taps_ref, gate_ref, fk_ref, fv_ref, prod_ref, raw):
    count = q_ref.shape[0]
    taps = taps_ref.shape[0]
    wide = count + EDGE
    blank = jnp.zeros((EDGE, LANES), jnp.float32)

    def run(reverse):
        feats = []
        for m, ref in enumerate((q_ref, k_ref, v_ref)):
            rim = rim_ref[m].astype(jnp.float32)
            raw[m, :EDGE] = rim[:EDGE]
            raw[m, EDGE : EDGE + count] = ref[...].astype(jnp.float32)
            raw[m, EDGE + count :] = rim[EDGE:]
            total = None
            for j in range(taps):
                start = j if reverse else EDGE - j
                term = taps_ref[j, m : m + 1, :] * raw[m, start : start + wide, :]
                total = term if total is None else total + term
            feats.append(jnp.concatenate([blank, total] if reverse else [total, blank], axis=0))
        gate_ref[0] = feats[0].astype(jnp.bfloat16)
        fk_ref[0] = feats[1]
        fv_ref[0] = feats[2]
        prod_ref[0] = (feats[1] * feats[2]).astype(jnp.bfloat16)

    for half in (0, 1):
        pl.when(pl.program_id(0) == half)(lambda half=half: run(half == 1))


def mix_kernel(prod_ref, low_ref, high_ref, gate_ref, stream_ref, base_ref, m_ref, head_ref, target_ref,
               mix_ref, lg_ref, a_ref, x, gated_s, logits):
    half, tile = pl.program_id(0), pl.program_id(1)
    tiles = pl.num_programs(1)
    count = stream_ref.shape[0]
    rows = prod_ref.shape[1]

    @pl.when((half == 0) & (tile == 0))
    def _():
        logits[...] = jnp.zeros_like(logits)

    def run(reverse):
        if reverse:
            x[:rows] = prod_ref[0]
            x[rows:] = high_ref[...]
        else:
            x[:BLOCK] = low_ref[...]
            x[BLOCK:] = prod_ref[0]
        banded(x, base_ref, mix_ref.at[0], reverse)
        first = rows - count if reverse else 0
        mix = mix_ref[0, first : first + count, :]
        gated = (gate_ref[0, first : first + count, :].astype(jnp.float32) * mix).astype(jnp.bfloat16)
        gated_s[half * tiles + tile] = gated
        m_high, m_low = split_bf16(m_ref[0])
        h_high, h_low = split_bf16(head_ref[0])
        stream = stream_ref[...]
        logits[...] += (mm(gated, m_high, 1, 1) + mm(gated, m_low, 1, 1)) + (
            mm(stream, h_high, 1, 1) + mm(stream, h_low, 1, 1))

    for side in (0, 1):
        pl.when(half == side)(lambda side=side: run(side == 1))

    @pl.when((half == 1) & (tile == tiles - 1))
    def _():
        lane = lax.broadcasted_iota(jnp.int32, logits.shape, 1)
        exponent = jnp.where(lane < 4, jnp.exp(logits[...]), 0.0)
        softmax_out = exponent / jnp.sum(exponent, axis=1, keepdims=True)
        grad = loss_scale * (softmax_out - jnp.where(lane == target_ref[...], 1.0, 0.0))
        lg_ref[...] = grad
        g_high, g_low = split_bf16(grad)

        @pl.loop(0, gated_s.shape[0])
        def _(i):
            block = gated_s[i]
            a_ref[i] = mm(g_high, block, 0, 0) + mm(g_low, block, 0, 0)


def grad_kernel(gate_ref, glow_ref, ghigh_ref, lg_ref, llow_ref, lhigh_ref, m_ref, mix_ref, fk_ref, fv_ref, base_ref,
                taps_ref, qo_ref, ko_ref, vo_ref, x, grads, pg, feat):
    count = lg_ref.shape[0]
    rows = gate_ref.shape[1]
    taps = taps_ref.shape[0]
    far = glow_ref.shape[0]

    def run(reverse):
        m_high, m_low = split_bf16(m_ref[0])
        if reverse:
            pieces = ((0, far, llow_ref[...], glow_ref[...]), (far, count, lg_ref[...], gate_ref[0, rows - count :, :]))
        else:
            pieces = ((0, count, lg_ref[...], gate_ref[0, :count, :]), (count, far, lhigh_ref[...], ghigh_ref[...]))
        for start, size, lg, gate in pieces:
            g_high, g_low = split_bf16(lg)
            part = mm(g_high, m_high) + (mm(g_high, m_low) + mm(g_low, m_high))
            grads[start : start + size] = part
            x[start : start + size] = (part * gate.astype(jnp.float32)).astype(jnp.bfloat16)
        banded(x, base_ref, pg, reverse)
        own = count + far - rows if reverse else 0
        feat[0] = grads[own : own + rows, :] * mix_ref[0]
        feat[1] = pg[...] * fv_ref[0]
        feat[2] = pg[...] * fk_ref[0]
        for m, out in enumerate((qo_ref, ko_ref, vo_ref)):
            total = None
            for j in range(taps):
                start = rows - count - j if reverse else j
                term = taps_ref[j, m : m + 1, :] * feat[m, start : start + count, :]
                total = term if total is None else total + term
            out[...] = total.astype(jnp.bfloat16)

    for side in (0, 1):
        pl.when(pl.program_id(0) == side)(lambda side=side: run(side == 1))


def per_device(query, key, value, stream, targets, short_filter, med_filter, out_weight, head):
    genomes, count, width = query.shape
    assert genomes == 1
    half = width // 2
    taps = short_filter.shape[0]
    tiles = half // LANES
    rows = count + 2 * EDGE
    far = count - 2 * EDGE
    groups = med_filter.shape[1]
    tile_groups = groups // tiles
    assert med_filter.shape[0] == BLOCK and BLOCK < rows <= 2 * BLOCK and rows + BLOCK == count + far and taps <= EDGE
    f32, bf16 = jnp.float32, jnp.bfloat16
    query, key, value, stream = (a.reshape(count, width) for a in (query, key, value, stream))
    seqs = lax.axis_size("seq")
    up = [(i, i + 1) for i in range(seqs - 1)]
    down = [(i + 1, i) for i in range(seqs - 1)]

    def to_right(a):
        return lax.ppermute(a, "seq", up)

    def to_left(a):
        return lax.ppermute(a, "seq", down)

    rim = jnp.concatenate([
        to_right(jnp.stack([a[count - EDGE :] for a in (query, key, value)])),
        to_left(jnp.stack([a[:EDGE] for a in (query, key, value)])),
    ], axis=1)

    head16 = jnp.pad(head, ((0, 12), (0, 0)))
    head2 = jnp.stack([head16, jnp.pad(head[::-1], ((0, 12), (0, 0)))])
    w_high = out_weight
    m_part = jnp.dot(head, w_high.T.astype(f32), precision=lax.Precision.HIGHEST)
    m_full = lax.all_gather(m_part, "fsdp", axis=1, tiled=True)
    m2 = jnp.stack([jnp.pad(m_full, ((0, 12), (0, 0))), jnp.pad(m_full[::-1], ((0, 12), (0, 0)))])

    table = med_filter.T.astype(f32)
    base = jnp.stack([
        jnp.pad(table[:, ::-1], ((0, 0), (1, BLOCK - 1))),
        jnp.pad(table, ((0, 0), (0, BLOCK))),
    ])

    sds = jax.ShapeDtypeStruct
    params = pltpu.CompilerParams(vmem_limit_bytes=VMEM_LIMIT, dimension_semantics=("arbitrary", "arbitrary"))
    whole = pl.BlockSpec((count, LANES), lambda h, t: (0, h * tiles + t))
    framed = pl.BlockSpec((1, rows, LANES), lambda h, t: (h, 0, t))
    taps_spec = pl.BlockSpec((taps, 3, LANES), lambda h, t: (0, 0, t))
    small = pl.BlockSpec((1, 16, LANES), lambda h, t: (h, 0, t))

    def fixed(*shape):
        return pl.BlockSpec(shape, lambda h, t: (0,) * len(shape))

    def low_side(size):
        return pl.BlockSpec((size, LANES), lambda h, t: (0, t * (1 - h) + (tiles - 1) * h))

    def high_side(size):
        return pl.BlockSpec((size, LANES), lambda h, t: (0, t * h))

    gate, feat_k, feat_v, prod = pl.pallas_call(
        featured_kernel,
        grid=(2, tiles),
        in_specs=[whole, whole, whole, pl.BlockSpec((3, 2 * EDGE, LANES), lambda h, t: (0, 0, h * tiles + t)), taps_spec],
        out_specs=[framed] * 4,
        out_shape=[sds((2, rows, half), bf16), sds((2, rows, half), f32), sds((2, rows, half), f32),
                   sds((2, rows, half), bf16)],
        scratch_shapes=[pltpu.VMEM((3, count + 2 * EDGE, LANES), f32)],
        compiler_params=params,
        cost_estimate=pl.CostEstimate(flops=14 * 3 * count * width, bytes_accessed=20 * count * width, transcendentals=0),
        name="featured",
    )(query, key, value, rim, short_filter)

    prod_low = to_right(prod[0, count - BLOCK : count])
    prod_high = to_left(prod[1, rows - count : rows - count + BLOCK])
    gate_high = to_left(gate[0, :far])
    gate_low = to_right(gate[1, rows - far :])

    mix, lg, a_part = pl.pallas_call(
        mix_kernel,
        grid=(2, tiles),
        in_specs=[framed, low_side(BLOCK), high_side(BLOCK), framed, whole,
                  pl.BlockSpec((1, tile_groups, 2 * BLOCK), lambda h, t: (h, t, 0)),
                  small, small, fixed(count, 1)],
        out_specs=[framed, fixed(count, 16), fixed(2 * tiles, 16, LANES)],
        out_shape=[sds((2, rows, half), f32), sds((count, 16), f32), sds((2 * tiles, 16, LANES), f32)],
        scratch_shapes=[pltpu.VMEM((rows + BLOCK, LANES), bf16), pltpu.VMEM((2 * tiles, count, LANES), bf16),
                        pltpu.VMEM((count, 16), f32)],
        compiler_params=params,
        cost_estimate=pl.CostEstimate(flops=512 * count * width * 8, bytes_accessed=12 * count * width, transcendentals=0),
        name="long_mix",
    )(prod, prod_low, prod_high, gate, stream, base, m2, head2, targets.reshape(count, 1))

    lg_high = to_left(lg[:far])
    lg_low = to_right(lg[count - far :])

    a_rows = a_part[:, :4].reshape(2, tiles, 4, LANES).transpose(0, 2, 1, 3).reshape(2, 4, half)
    a_sum = lax.psum(a_rows[0] + a_rows[1, ::-1], ("fsdp", "seq"))

    query_grad, key_grad, value_grad = pl.pallas_call(
        grad_kernel,
        grid=(2, tiles),
        in_specs=[framed, low_side_far(far, tiles), high_side_far(far, tiles), fixed(count, 16), fixed(far, 16),
                  fixed(far, 16), small, framed, framed, framed,
                  pl.BlockSpec((1, tile_groups, 2 * BLOCK), lambda h, t: (1 - h, t, 0)), taps_spec],
        out_specs=[whole] * 3,
        out_shape=[sds((count, width), bf16)] * 3,
        scratch_shapes=[pltpu.VMEM((count + far, LANES), bf16), pltpu.VMEM((count + far, LANES), f32),
                        pltpu.VMEM((rows, LANES), f32), pltpu.VMEM((3, rows, LANES), f32)],
        compiler_params=params,
        cost_estimate=pl.CostEstimate(flops=512 * count * width * 8, bytes_accessed=24 * count * width, transcendentals=0),
        name="input_grads",
    )(gate, gate_low, gate_high, lg, lg_low, lg_high, m2, mix, feat_k, feat_v, base, short_filter)

    own = out_weight.shape[0]
    mine = lax.dynamic_slice_in_dim(a_sum, lax.axis_index("fsdp") * own, own, axis=1) / loss_scale
    out_grad = sum(mine[v][:, None] * head[v][None, :] for v in range(head.shape[0]))
    return (query_grad[None], key_grad[None], value_grad[None], out_grad)


def low_side_far(size, tiles):
    return pl.BlockSpec((size, LANES), lambda h, t: (0, t * h))


def high_side_far(size, tiles):
    return pl.BlockSpec((size, LANES), lambda h, t: (0, t * (1 - h) + (tiles - 1) * h))


def solution(mesh):
    rows = P("fsdp", "seq", None)
    return jax.shard_map(
        per_device,
        mesh=mesh,
        in_specs=(rows, rows, rows, rows, P("fsdp", "seq"), P(), P(), P("fsdp", None), P()),
        out_specs=(rows, rows, rows, P("fsdp", None)),
        check_vma=False,
    )
```

time: 424 us -> 187 us (0.44)
  the two profiles are of different devices: /device:TPU:0 before, /device:TPU:1 now
where the time goes in v1:
time: 187 us; the launch traced here: 185 us
  Pallas kernels  57.5 us (31%)
  blocking collectives  54 us (29%)
  local copies, waits for them, and re-layouts  35.5 us (19%)
  starting transfers between devices  26.2 us (14%)
  other arithmetic  8.33 us (4%)
  matrix products  2.48 us (1%)
    psum x1, blocking collectives, per_device(): a_sum = lax.psum(a_rows[0] + a_rows[1, ::-1], ('fsdp', 'seq'))  43.3 us
    pallas_call x1, Pallas kernels, per_device(): pl.pallas_call(grad_kernel, grid=(2, tiles), in_specs=[framed, low_side_f...  25.2 us
    pallas_call x1, Pallas kernels, per_device(): pl.pallas_call(mix_kernel, grid=(2, tiles), in_specs=[framed, low_side(BL...  19.8 us
    ppermute x4, starting transfers between devices, to_right(): return lax.ppermute(a, 'seq', up)  14.7 us
    pallas_call x1, Pallas kernels, per_device(): pl.pallas_call(featured_kernel, grid=(2, tiles), in_specs=[whole, whole,...  12.6 us
    ppermute x4, starting transfers between devices, to_left(): return lax.ppermute(a, 'seq', down)  11.5 us
    unnamed x44, local copies, waits for them, and re-layouts  11.3 us
    all_gather x1, blocking collectives, per_device(): m_full = lax.all_gather(m_part, 'fsdp', axis=1, tiled=True)  10.7 us
  transfers between devices with their start and end apart: 8, of which 0 were waited for; matrix products, arithmetic and copies ran while one was open for 16% of the time, Pallas kernels for 11%

profile of v1, /device:TPU:1, one launch (start us, length us, event | category | flops | bytes accessed | tf_op | source)
XLA Modules:
  0.0 185.0 jit_solution(10881844225112864565)
XLA Ops:
  0.6 0.0 copy-start
  0.6 0.0 copy-start.18
  0.7 0.0 copy-start.20
  0.7 0.0 copy-start.19
  0.7 1.0 fusion.2
  1.7 1.0 fusion
  2.7 2.0 %collective-permute-start.1 = (bf16[3,8,4096]{2,1,0:T(8,128)(2,1)S(1)}, bf16[3,8,4096]{2,1,0:T(8,128)(2,1)S(1)}, u32[]{:S(2)}, u32[]{:S(2)}) collective-permute-start(bf16[3,8,4096]{2,1,0:T(8,128)(2,1)S(1)} %pad_maximum_fusion.5), channel_id=1, source_target_pairs={{4,0},{8,4},{12,8},{16,12},{20,16},{24,20},{28,24},{5,1},{9,5},{13... | collective-permute-start | bytes 589832 | tf_op jit(solution)/shard_map/ppermute | solution.py:185
  4.7 4.5 %collective-permute-start = (bf16[3,8,4096]{2,1,0:T(8,128)(2,1)S(1)}, bf16[3,8,4096]{2,1,0:T(8,128)(2,1)S(1)}, u32[]{:S(2)}, u32[]{:S(2)}) collective-permute-start(bf16[3,8,4096]{2,1,0:T(8,128)(2,1)S(1)} %pad_maximum_fusion.4), channel_id=1, source_target_pairs={{0,4},{4,8},{8,12},{12,16},{16,20},{20,24},{24,28},{1,5},{5,9},{9,... | collective-permute-start | bytes 589832 | tf_op jit(solution)/shard_map/ppermute | solution.py:182
  9.2 5.6 %rev.14 = f32[4,2048]{1,0:T(4,128)S(1)} reverse(f32[4,2048]{1,0:T(4,128)} %param.17), dimensions={0} | reverse | bytes 65536 | tf_op jit(solution)/shard_map/rev | solution.py:193
  14.8 1.6 fusion.5
  16.4 0.0 copy-done
  16.4 2.5 %fusion.7 = f32[4,512]{1,0:T(4,128)S(1)} fusion(f32[4,2048]{1,0:T(4,128)} %param.17, bf16[512,2048]{1,0:T(8,128)(2,1)S(1)} %copy-done), kind=kOutput, calls=%fused_computation.27 | convolution fusion | flops 50331648 | bytes 2138112 | tf_op jit(solution)/shard_map/dot_general | solution.py:195
  18.9 10.7 %all_gather.3 = f32[4,2048]{1,0:T(4,128)S(1)} all-gather(f32[4,512]{1,0:T(4,128)S(1)} %fusion.7), channel_id=1, replica_groups=mesh['seq'=8,'fsdp'=4] {'fsdp'}, dimensions={1}, use_global_device_ids=true | all-gather | bytes 40960 | tf_op jit(solution)/shard_map/all_gather | solution.py:196
  29.5 0.4 rev.13
  29.9 0.1 copy.17
  30.0 0.1 rev.12
  30.1 0.1 pad_bitcast_fusion.4
  30.3 0.1 copy.16.taps_ref
  30.5 0.8 pad_maximum_fusion.2.m_ref
  31.2 0.7 pad_maximum_fusion.3.head_ref
  31.9 0.0 collective-permute-done.1
  31.9 0.0 collective-permute-done
  32.0 0.0 copy-start.5
  32.0 1.3 copy-done.5
  33.3 1.3 copy-done.6
  34.6 1.3 copy-done.7
  35.9 12.6 %featured.1 = (bf16[2,176,2048]{2,1,0:T(8,128)(2,1)S(1)}, f32[2,176,2048]{2,1,0:T(8,128)}, f32[2,176,2048]{2,1,0:T(8,128)}, bf16[2,176,2048]{2,1,0:T(8,128)(2,1)}) custom-call(bf16[160,4096]{1,0:T(8,128)(2,1)S(1)} %bitcast.47, bf16[160,4096]{1,0:T(8,128)(2,1)S(1)} %bitcast.48, bf16[160,4096]{1,0:T(8,128)(2,1)S(1)} %bitcast.49, ...), custom_call_target="tpu_custom_call" | custom-call | flops 27525120 | bytes 13107200 | tf_op jit(solution)/shard_map/featured/pallas_call | solution.py:221
  48.5 2.8 %slice_bitcast_fusion.2 = (bf16[128,2048]{1,0:T(8,128)(2,1)}, bf16[128,2048]{1,0:T(8,128)(2,1)}) fusion(bf16[2,176,2048]{2,1,0:T(8,128)(2,1)} %get-tuple-element.15.prod_ref), kind=kLoop, calls=%fused_computation.3 | loop fusion | bytes 2097152 | tf_op jit(solution)/shard_map/squeeze | solution.py:235
  51.3 4.0 %collective-permute-start.5 = (bf16[128,2048]{1,0:T(8,128)(2,1)}, bf16[128,2048]{1,0:T(8,128)(2,1)}, u32[]{:S(2)}, u32[]{:S(2)}) collective-permute-start(bf16[128,2048]{1,0:T(8,128)(2,1)} %get-tuple-element.24), channel_id=1, source_target_pairs={{4,0},{8,4},{12,8},{16,12},{20,16},{24,20},{28,24},{5,1},{9,5},{13... | collective-permute-start | bytes 1572872 | tf_op jit(solution)/shard_map/ppermute | solution.py:185
  55.3 3.0 %collective-permute-start.4 = (bf16[128,2048]{1,0:T(8,128)(2,1)}, bf16[128,2048]{1,0:T(8,128)(2,1)}, u32[]{:S(2)}, u32[]{:S(2)}) collective-permute-start(bf16[128,2048]{1,0:T(8,128)(2,1)} %get-tuple-element.25), channel_id=1, source_target_pairs={{0,4},{4,8},{8,12},{12,16},{16,20},{20,24},{24,28},{1,5},{5,9},{9,... | collective-permute-start | bytes 1572872 | tf_op jit(solution)/shard_map/ppermute | solution.py:182
  58.3 0.7 pad_maximum_fusion.1.base_ref
  59.1 1.4 copy.18.target_ref
  60.5 1.1 slice_bitcast_fusion
  61.6 2.1 %collective-permute-start.3 = (bf16[144,2048]{1,0:T(8,128)(2,1)}, bf16[144,2048]{1,0:T(8,128)(2,1)}, u32[]{:S(2)}, u32[]{:S(2)}) collective-permute-start(bf16[144,2048]{1,0:T(8,128)(2,1)} %get-tuple-element.26), channel_id=1, source_target_pairs={{4,0},{8,4},{12,8},{16,12},{20,16},{24,20},{28,24},{5,1},{9,5},{13... | collective-permute-start | bytes 1769480 | tf_op jit(solution)/shard_map/ppermute | solution.py:185
  63.7 3.5 %collective-permute-start.2 = (bf16[144,2048]{1,0:T(8,128)(2,1)}, bf16[144,2048]{1,0:T(8,128)(2,1)}, u32[]{:S(2)}, u32[]{:S(2)}) collective-permute-start(bf16[144,2048]{1,0:T(8,128)(2,1)} %get-tuple-element.27), channel_id=1, source_target_pairs={{0,4},{4,8},{8,12},{12,16},{16,20},{20,24},{24,28},{1,5},{5,9},{9,... | collective-permute-start | bytes 1769480 | tf_op jit(solution)/shard_map/ppermute | solution.py:182
  67.1 0.0 collective-permute-done.5.high_ref
  67.2 0.0 collective-permute-done.4.low_ref
  67.2 0.0 copy-done.1
  67.2 0.0 copy-start.8
  67.2 0.9 copy-done.8
  68.1 0.9 copy-done.10
  69.1 1.4 copy-done.12
  70.4 0.9 copy-done.15
  71.4 0.9 copy-done.16
  72.3 1.3 copy-done.17
  73.6 19.8 %long_mix.1 = (f32[2,176,2048]{2,1,0:T(8,128)}, f32[160,16]{1,0:T(8,128)S(1)}, f32[16,16,256]{2,1,0:T(8,128)S(1)}) custom-call(bf16[2,176,2048]{2,1,0:T(8,128)(2,1)S(1)} %copy-done.12, bf16[128,2048]{1,0:T(8,128)(2,1)} %collective-permute-done.4.low_ref, bf16[128,2048]{1,0:T(8,128)(2,1)} %collective-permute-done.5.high_ref, bf16[2,176,2048]{2,1,0:T(8,128)(2,1)} %copy-done.1, ...), custom_call_target="tpu_custom_call" | custom-call | flops 2684354560 | bytes 7864320 | tf_op jit(solution)/shard_map/long_mix/pallas_call | solution.py:239
  93.4 0.6 copy-done.13
  94.0 0.6 fusion.4
  94.7 7.5 %rev.15 = f32[1,4,2048]{2,1,0:T(4,128)} reverse(f32[1,4,2048]{2,1,0:T(4,128)} %bitcast.53), dimensions={1} | reverse | bytes 65536 | tf_op jit(solution)/shard_map/rev | solution.py:258
  102.2 1.4 bitcast_add_fusion
  103.6 43.3 %psum.7 = f32[4,2048]{1,0:T(4,128)} all-reduce(f32[4,2048]{1,0:T(4,128)} %bitcast_add_fusion), channel_id=1, replica_groups=mesh['seq'=8,'fsdp'=4] {'fsdp','seq'}, use_global_device_ids=true, to_apply=%region_0.1 | all-reduce | flops 8192 | bytes 65536 | tf_op jit(solution)/shard_map/psum | solution.py:258
  146.9 1.0 fusion.3
  147.9 0.7 dynamic-slice_multiply_fusion
  148.7 3.4 %collective-permute-start.7 = (f32[144,16]{1,0:T(8,128)S(1)}, f32[144,16]{1,0:T(8,128)S(1)}, u32[]{:S(2)}, u32[]{:S(2)}) collective-permute-start(f32[144,16]{1,0:T(8,128)S(1)} %get-tuple-element.34), channel_id=1, source_target_pairs={{4,0},{8,4},{12,8},{16,12},{20,16},{24,20},{28,24},{5,1},{9,5},{13... | collective-permute-start | bytes 27656 | tf_op jit(solution)/shard_map/ppermute | solution.py:185
  152.1 3.8 %collective-permute-start.6 = (f32[144,16]{1,0:T(8,128)S(1)}, f32[144,16]{1,0:T(8,128)S(1)}, u32[]{:S(2)}, u32[]{:S(2)}) collective-permute-start(f32[144,16]{1,0:T(8,128)S(1)} %get-tuple-element.35), channel_id=1, source_target_pairs={{0,4},{4,8},{8,12},{12,16},{16,20},{20,24},{24,28},{1,5},{5,9},{9,... | collective-permute-start | bytes 27656 | tf_op jit(solution)/shard_map/ppermute | solution.py:182
  155.9 3.9 %multiply_add_fusion = f32[512,2048]{1,0:T(8,128)} fusion(f32[2048]{0:T(1024)} %bitcast.56, f32[512]{0:T(512)S(1)} %bitcast.59, f32[2048]{0:T(1024)} %bitcast.57, f32[512]{0:T(512)S(1)} %bitcast.60, f32[2048]{0:T(1024)S(1)} %bitcast.55, f32[512]{0:T(512)S(1)} %bitcast.61, f32[2048]{0:T(1024)S(1)} %bitcast.54, f32[512]{0:T(512)S(1)} %bitcast.58), kind=kLoop, calls=%fused_computation | loop fusion | flops 7340032 | bytes 4235264 | tf_op jit(solution)/shard_map/add | solution.py:277
  159.8 0.0 collective-permute-done.7.lhigh_ref
  159.8 0.0 collective-permute-done.6.llow_ref
  159.8 0.0 collective-permute-done.3.ghigh_ref
  159.8 0.0 collective-permute-done.2.glow_ref
  159.8 0.0 copy-done.2
  159.8 0.0 copy-done.4
  159.8 0.0 copy-done.9
  159.9 25.2 %input_grads.1 = (bf16[160,4096]{1,0:T(8,128)(2,1)}, bf16[160,4096]{1,0:T(8,128)(2,1)}, bf16[160,4096]{1,0:T(8,128)(2,1)}) custom-call(bf16[2,176,2048]{2,1,0:T(8,128)(2,1)S(1)} %copy-done.2, bf16[144,2048]{1,0:T(8,128)(2,1)} %collective-permute-done.2.glow_ref, bf16[144,2048]{1,0:T(8,128)(2,1)} %collective-permute-done.3.ghigh_ref, ...), custom_call_target="tpu_custom_call" | custom-call | flops 2684354560 | bytes 15728640 | tf_op jit(solution)/shard_map/input_grads/pallas_call | solution.py:260
  (29 shorter events, 0.2 us)
Async XLA Ops:
  0.6 15.8 %copy-start = (bf16[512,2048]{1,0:T(8,128)(2,1)S(1)}, bf16[512,2048]{1,0:T(8,128)(2,1)}, u32[]{:S(2)}) copy-start(bf16[512,2048]{1,0:T(8,128)(2,1)} %param.16) | copy-start | bytes 6291460
  0.6 29.8 %copy-start.18 = (f32[4,2048]{1,0:T(4,128)S(1)}, f32[4,2048]{1,0:T(4,128)}, u32[]{:S(2)}) copy-start(f32[4,2048]{1,0:T(4,128)} %param.17) | copy-start | bytes 98308
  0.7 29.2 %copy-start.20 = (bf16[128,128]{1,0:T(8,128)(2,1)S(1)}, bf16[128,128]{1,0:T(8,128)(2,1)}, u32[]{:S(2)}) copy-start(bf16[128,128]{1,0:T(8,128)(2,1)} %param.15) | copy-start | bytes 98308
  0.7 29.6 %copy-start.19 = (f32[7,3,2048]{2,0,1:T(8,128)S(1)}, f32[7,3,2048]{2,0,1:T(8,128)}, u32[]{:S(2)}) copy-start(f32[7,3,2048]{2,0,1:T(8,128)} %param.14) | copy-start | bytes 516100
  2.7 29.2 %collective-permute-start.1 = (bf16[3,8,4096]{2,1,0:T(8,128)(2,1)S(1)}, bf16[3,8,4096]{2,1,0:T(8,128)(2,1)S(1)}, u32[]{:S(2)}, u32[]{:S(2)}) collective-permute-start(bf16[3,8,4096]{2,1,0:T(8,128)(2,1)S(1)} %pad_maximum_fusion.5), channel_id=1, source_target_pairs={{4,0},{8,4},{12,8},{16,12},{20,16},{24,20},{28,24},{5,1},{9,5},{13... | collective-permute-start | bytes 589832 | tf_op jit(solution)/shard_map/ppermute | solution.py:185
  4.7 27.2 %collective-permute-start = (bf16[3,8,4096]{2,1,0:T(8,128)(2,1)S(1)}, bf16[3,8,4096]{2,1,0:T(8,128)(2,1)S(1)}, u32[]{:S(2)}, u32[]{:S(2)}) collective-permute-start(bf16[3,8,4096]{2,1,0:T(8,128)(2,1)S(1)} %pad_maximum_fusion.4), channel_id=1, source_target_pairs={{0,4},{4,8},{8,12},{12,16},{16,20},{20,24},{24,28},{1,5},{5,9},{9,... | collective-permute-start | bytes 589832 | tf_op jit(solution)/shard_map/ppermute | solution.py:182
  30.4 18.1 %copy-start.3 = (f32[7,3,2048]{2,1,0:T(4,128)}, f32[7,3,2048]{2,1,0:T(4,128)S(1)}, u32[]{:S(2)}) copy-start(f32[7,3,2048]{2,1,0:T(4,128)S(1)} %copy.16.taps_ref) | copy-start | bytes 516100
  32.0 1.3 copy-start.5
  33.3 1.3 copy-start.6
  34.6 1.3 copy-start.7
  48.5 18.7 %copy-start.1 = (bf16[2,176,2048]{2,1,0:T(8,128)(2,1)}, bf16[2,176,2048]{2,1,0:T(8,128)(2,1)S(1)}, u32[]{:S(2)}) copy-start(bf16[2,176,2048]{2,1,0:T(8,128)(2,1)S(1)} %get-tuple-element.14.gate_ref) | copy-start | bytes 4325380
  51.3 15.8 %collective-permute-start.5 = (bf16[128,2048]{1,0:T(8,128)(2,1)}, bf16[128,2048]{1,0:T(8,128)(2,1)}, u32[]{:S(2)}, u32[]{:S(2)}) collective-permute-start(bf16[128,2048]{1,0:T(8,128)(2,1)} %get-tuple-element.24), channel_id=1, source_target_pairs={{4,0},{8,4},{12,8},{16,12},{20,16},{24,20},{28,24},{5,1},{9,5},{13... | collective-permute-start | bytes 1572872 | tf_op jit(solution)/shard_map/ppermute | solution.py:185
  55.3 11.8 %collective-permute-start.4 = (bf16[128,2048]{1,0:T(8,128)(2,1)}, bf16[128,2048]{1,0:T(8,128)(2,1)}, u32[]{:S(2)}, u32[]{:S(2)}) collective-permute-start(bf16[128,2048]{1,0:T(8,128)(2,1)} %get-tuple-element.25), channel_id=1, source_target_pairs={{0,4},{4,8},{8,12},{12,16},{16,20},{20,24},{24,28},{1,5},{5,9},{9,... | collective-permute-start | bytes 1572872 | tf_op jit(solution)/shard_map/ppermute | solution.py:182
  61.6 98.2 %collective-permute-start.3 = (bf16[144,2048]{1,0:T(8,128)(2,1)}, bf16[144,2048]{1,0:T(8,128)(2,1)}, u32[]{:S(2)}, u32[]{:S(2)}) collective-permute-start(bf16[144,2048]{1,0:T(8,128)(2,1)} %get-tuple-element.26), channel_id=1, source_target_pairs={{4,0},{8,4},{12,8},{16,12},{20,16},{24,20},{28,24},{5,1},{9,5},{13... | collective-permute-start | bytes 1769480 | tf_op jit(solution)/shard_map/ppermute | solution.py:185
  63.7 96.1 %collective-permute-start.2 = (bf16[144,2048]{1,0:T(8,128)(2,1)}, bf16[144,2048]{1,0:T(8,128)(2,1)}, u32[]{:S(2)}, u32[]{:S(2)}) collective-permute-start(bf16[144,2048]{1,0:T(8,128)(2,1)} %get-tuple-element.27), channel_id=1, source_target_pairs={{0,4},{4,8},{8,12},{12,16},{16,20},{20,24},{24,28},{1,5},{5,9},{9,... | collective-permute-start | bytes 1769480 | tf_op jit(solution)/shard_map/ppermute | solution.py:182
  67.2 1.0 copy-start.8
  68.1 0.9 copy-start.10
  69.1 1.4 copy-start.12
  70.4 0.9 copy-start.15
  71.4 0.9 copy-start.16
  72.3 1.3 copy-start.17
  93.4 0.6 copy-start.13
  94.0 65.8 %copy-start.2 = (bf16[2,176,2048]{2,1,0:T(8,128)(2,1)S(1)}, bf16[2,176,2048]{2,1,0:T(8,128)(2,1)}, u32[]{:S(2)}) copy-start(bf16[2,176,2048]{2,1,0:T(8,128)(2,1)} %copy-done.1) | copy-start | bytes 4325380
  146.9 12.9 %copy-start.4 = (f32[7,3,2048]{2,1,0:T(4,128)S(1)}, f32[7,3,2048]{2,1,0:T(4,128)}, u32[]{:S(2)}) copy-start(f32[7,3,2048]{2,1,0:T(4,128)} %copy-done.3) | copy-start | bytes 516100
  146.9 12.9 %copy-start.9 = (f32[2,16,2048]{2,1,0:T(8,128)S(1)}, f32[2,16,2048]{2,1,0:T(8,128)}, u32[]{:S(2)}) copy-start(f32[2,16,2048]{2,1,0:T(8,128)} %pad_maximum_fusion.2.m_ref) | copy-start | bytes 786436
  146.9 12.9 %copy-start.11 = (f32[2,128,256]{2,1,0:T(8,128)S(1)}, f32[2,128,256]{2,1,0:T(8,128)}, u32[]{:S(2)}) copy-start(f32[2,128,256]{2,1,0:T(8,128)} %pad_maximum_fusion.1.base_ref) | copy-start | bytes 786436
  146.9 12.9 %copy-start.14 = (f32[160,16]{1,0:T(8,128)S(1)}, f32[160,16]{1,0:T(8,128)}, u32[]{:S(2)}) copy-start(f32[160,16]{1,0:T(8,128)} %copy-done.13) | copy-start | bytes 30724
  148.7 11.1 %collective-permute-start.7 = (f32[144,16]{1,0:T(8,128)S(1)}, f32[144,16]{1,0:T(8,128)S(1)}, u32[]{:S(2)}, u32[]{:S(2)}) collective-permute-start(f32[144,16]{1,0:T(8,128)S(1)} %get-tuple-element.34), channel_id=1, source_target_pairs={{4,0},{8,4},{12,8},{16,12},{20,16},{24,20},{28,24},{5,1},{9,5},{13... | collective-permute-start | bytes 27656 | tf_op jit(solution)/shard_map/ppermute | solution.py:185
  152.1 7.7 %collective-permute-start.6 = (f32[144,16]{1,0:T(8,128)S(1)}, f32[144,16]{1,0:T(8,128)S(1)}, u32[]{:S(2)}, u32[]{:S(2)}) collective-permute-start(f32[144,16]{1,0:T(8,128)S(1)} %get-tuple-element.35), channel_id=1, source_target_pairs={{0,4},{4,8},{8,12},{12,16},{16,20},{20,24},{24,28},{1,5},{5,9},{9,... | collective-permute-start | bytes 27656 | tf_op jit(solution)/shard_map/ppermute | solution.py:182

commit v2 on v1

v2 whole, which is shorter than its diff:
```python
import functools

import jax
import jax.numpy as jnp
from jax import lax
from jax.experimental import pallas as pl
from jax.experimental.pallas import tpu as pltpu
from jax.sharding import PartitionSpec as P

loss_scale = 64.0
LANES = 256
PART = 128
EDGE = 8
RIM = 16
ROWS = 96
NUC = 4
MESH = pl.DeviceIdType.MESH
VMEM_LIMIT = 58 * 1024 * 1024
f32, bf16 = jnp.float32, jnp.bfloat16


def split_bf16(x):
    high = x.astype(bf16)
    low = (x - high.astype(f32)).astype(bf16)
    return high, low


def mm(a, b, ca=1, cb=0):
    return lax.dot_general(a, b, (((ca,), (cb,)), ((), ())), preferred_element_type=f32)


def short_conv(taps, x, first, step, size):
    near = far = None
    for j in range(4):
        moved = x(first + step * j, size)
        term = taps[j] * moved
        near = term if near is None else near + term
        if j + 4 < len(taps):
            term = taps[j + 4] * moved
            far = term if far is None else far + term
    return near, far


def placed(size, reverse, source):
    r = lax.broadcasted_iota(jnp.int32, (size, 16), 0)
    c = lax.broadcasted_iota(jnp.int32, (size, 16), 1)
    v = r % 16
    row = (3 - v if reverse else v) + source(r // 16)
    return jnp.where((v < 4) & (c == row), 1.0, 0.0).astype(bf16)


def block_kernel(
    sizes, q_hbm, k_hbm, v_hbm, stream_hbm, target_ref, taps_ref, med_ref, w_hbm, head_ref,
    qo_ref, ko_ref, vo_ref, a_ref,
    q_ref, k_ref, v_ref, stream_ref, w_ref, done,
    rim_low, rim_high, raw, gate, prod, prod_low, prod_high, gate_low, gate_high, feat_k, feat_v, mix, toep,
    x, gated_s, logits, lg, lg_low, lg_high, head8, m_all, m_full, m_cat, n_cat, coef, grads, pg, feat, a_own, a_in,
    b_in, b_own,
    in_sems, out_sems, rim_ss, rim_rs, prod_ss, prod_rs, gate_ss, gate_rs, lg_ss, lg_rs, m_ss, m_rs, a_ss, a_rs,
    b_ss, b_rs,
):
    seqs, shards = sizes
    s, f = lax.axis_index("seq"), lax.axis_index("fsdp")
    count, width = q_ref.shape
    half = width // 2
    tiles = half // LANES
    rows = gate.shape[1]
    far = gate_low.shape[0]
    taps_n = taps_ref.shape[1]
    own = w_ref.shape[0]
    has_left, has_right = s > 0, s < seqs - 1
    loads = [
        pltpu.make_async_copy(src, dst, in_sems.at[i])
        for i, (src, dst) in enumerate(
            ((w_hbm, w_ref), (q_hbm, q_ref), (k_hbm, k_ref), (v_hbm, v_ref), (stream_hbm, stream_ref)))
    ]
    for load in loads:
        load.start()
    left, right = (s - 1, f), (s + 1, f)

    def seq_peer(d):
        return lax.rem(s + d, seqs)

    def shard_peer(d):
        return lax.rem(f + d, shards)

    barrier = pltpu.get_barrier_semaphore()
    for d in range(1, seqs):
        pl.semaphore_signal(barrier, inc=1, device_id=(seq_peer(d), f), device_id_type=MESH)
    for d in range(1, shards):
        pl.semaphore_signal(barrier, inc=1, device_id=(s, shard_peer(d)), device_id_type=MESH)
    pl.semaphore_wait(barrier, seqs + shards - 2)

    def send(src, dst, ss, rs, to):
        return pltpu.make_async_remote_copy(src_ref=src, dst_ref=dst, send_sem=ss, recv_sem=rs, device_id=to,
                                            device_id_type=MESH)

    def cols(t):
        return pl.ds(pl.multiple_of(t * LANES, LANES), LANES)

    def rim_copy(side, m):
        ref = (q_hbm, k_hbm, v_hbm)[m]
        if side == 0:
            return send(ref.at[count - RIM :], rim_low.at[m], rim_ss.at[side, m], rim_rs.at[side, m], right)
        return send(ref.at[:RIM], rim_high.at[m], rim_ss.at[side, m], rim_rs.at[side, m], left)

    def prod_copy(side, t):
        if side == 0:
            return send(prod.at[0, count - PART : count, cols(t)], prod_low.at[:, cols(t)], prod_ss.at[side, t],
                        prod_rs.at[side, t], right)
        return send(prod.at[1, rows - count : rows - count + PART, cols(t)], prod_high.at[:, cols(t)],
                    prod_ss.at[side, t], prod_rs.at[side, t], left)

    def gate_copy(side, t):
        if side == 0:
            return send(gate.at[1, rows - far :, cols(t)], gate_low.at[:, cols(t)], gate_ss.at[side, t],
                        gate_rs.at[side, t], right)
        return send(gate.at[0, :far, cols(t)], gate_high.at[:, cols(t)], gate_ss.at[side, t], gate_rs.at[side, t], left)

    def lg_copy(side):
        if side == 0:
            return send(lg.at[count - far :], lg_low, lg_ss.at[side], lg_rs.at[side], right)
        return send(lg.at[:far], lg_high, lg_ss.at[side], lg_rs.at[side], left)

    sends = (has_right, has_left)
    gets = (has_left, has_right)

    def start(side, copy):
        pl.when(sends[side])(lambda: copy.start())

    def sent(side, copy):
        pl.when(sends[side])(lambda: copy.wait_send())

    def arrived(side, copy):
        pl.when(gets[side])(lambda: copy.wait_recv())

    def clear(refs, absent):
        @pl.when(absent)
        def _():
            for ref in refs:
                ref[...] = jnp.zeros_like(ref)

    for side in (0, 1):
        for m in range(3):
            start(side, rim_copy(side, m))
    clear((rim_low, prod_low, gate_low, lg_low), s == 0)
    clear((rim_high, prod_high, gate_high, lg_high), s == seqs - 1)

    head8[...] = jnp.zeros_like(head8)
    head8[: head_ref.shape[0]] = head_ref[...]

    def stacked(value):
        high, low = split_bf16(value)
        return jnp.concatenate([high.astype(f32), low.astype(f32)], axis=0).astype(bf16)

    h_cat = stacked(head8[...])
    loads[0].wait()
    both = mm(h_cat, w_ref[...], 1, 1)
    m_all[f] = both[:8] + both[8:]

    def m_copy(d, slot):
        return send(m_all.at[f], m_all.at[slot], m_ss.at[d - 1], m_rs.at[slot], (s, shard_peer(d)))

    for d in range(1, shards):
        m_copy(d, f).start()

    med = med_ref[...]
    tap = lax.broadcasted_iota(jnp.int32, (PART, 2 * PART), 0)
    place = lax.broadcasted_iota(jnp.int32, (PART, 2 * PART), 1)
    for o, here in enumerate((place == PART - tap, place == tap)):
        grads[:PART, :] = mm(med, jnp.where(here, 1.0, 0.0).astype(bf16), 0, 0)

        @pl.loop(0, toep.shape[1])
        def _(i):
            base = grads[pl.ds(pl.multiple_of(i * 8, 8), 8), :]
            for g in range(8):
                row = jnp.broadcast_to(base[g : g + 1, :], (ROWS, 2 * PART))
                toep[o, i, g * ROWS : (g + 1) * ROWS, :] = pltpu.roll(row, 0, 1, stride=1, stride_axis=0).astype(bf16)

    def banded(o, t, x, out_ref, slot):
        span = ROWS + PART
        late = rows - ROWS
        lane = lax.rem(lax.broadcasted_iota(jnp.int32, (1, 2 * PART), 1), PART) // (PART // 8)
        for part in range(LANES // PART):
            here = slice(part * PART, (part + 1) * PART)
            two = jnp.concatenate([x[:span, here], x[late : late + span, here]], axis=1)
            every = mm(toep[o, t * (LANES // PART) + part, :, :span], two)
            got = every[:ROWS]
            for g in range(1, 8):
                got = jnp.where(lane == g, every[g * ROWS : (g + 1) * ROWS], got)
            out_ref[slot, :ROWS, here] = got[:, :PART]
            out_ref[slot, late:, here] = got[:, PART:]

    def low_half(i):
        return jnp.where(i == 1, 8, 0)

    for h in (0, 1):
        n_cat[h] = mm(placed(32, h == 1, low_half), h_cat).astype(bf16)

    for load in loads[1:]:
        load.wait()
    for side in (0, 1):
        for m in range(3):
            arrived(side, rim_copy(side, m))

    for h in (0, 1):
        blank = jnp.zeros((EDGE, LANES), f32)

        def featured(t, raw):
            there = pl.ds(pl.multiple_of(h * half + t * LANES, LANES), LANES)
            feats = []
            for m, ref in enumerate((q_ref, k_ref, v_ref)):
                raw[m, :RIM] = rim_low[m, :, there].astype(f32)
                raw[m, RIM : RIM + count] = ref[:, there].astype(f32)
                raw[m, RIM + count :] = rim_high[m, :, there].astype(f32)
                taps = [taps_ref[m, j : j + 1, cols(t)] for j in range(taps_n)]
                near, away = short_conv(taps, lambda a, n: raw[m, a : a + n, :], EDGE, 1 if h else -1, rows)
                if h:
                    value = jnp.concatenate([blank, near[: rows - EDGE] + away[4 : rows - 4]], axis=0)
                else:
                    value = jnp.concatenate([near[EDGE:] + away[4 : rows - 4], blank], axis=0)
                feats.append(value)
            gate[h, :, cols(t)] = feats[0].astype(bf16)
            feat_k[h, :, cols(t)] = feats[1]
            feat_v[h, :, cols(t)] = feats[2]
            prod[h, :, cols(t)] = (feats[1] * feats[2]).astype(bf16)

        @pl.loop(0, tiles // 2)
        def _(i):
            for u in (0, 1):
                featured(2 * i + u, raw.at[u])
            for u in (0, 1):
                start(h, prod_copy(h, 2 * i + u))
                start(1 - h, gate_copy(1 - h, 2 * i + u))

    for d in range(1, shards):
        m_copy(d, shard_peer(d)).wait_recv()
    for p in range(shards):
        m_full[:, p * own : (p + 1) * own] = m_all[p]
    both_m = stacked(m_full[...])
    for h in (0, 1):
        m_cat[h] = mm(placed(48, h == 1, low_half), both_m).astype(bf16)

    logits[...] = jnp.zeros_like(logits)
    for h in (0, 1):

        def mixed(t, x):
            if h:
                x[:rows] = prod[1, :, cols(t)]
                x[rows:] = prod_high[:, cols(t)]
            else:
                x[:PART] = prod_low[:, cols(t)]
                x[PART:] = prod[0, :, cols(t)]
            banded(h, t, x, mix, h * tiles + t)
            first = rows - count if h else 0
            gated = (gate[h, first : first + count, cols(t)].astype(f32)
                     * mix[h * tiles + t, first : first + count, :]).astype(bf16)
            gated_s[h * tiles + t] = gated
            stream = stream_ref[:, pl.ds(pl.multiple_of(h * half + t * LANES, LANES), LANES)]
            return mm(gated, m_cat[h, :32, cols(t)], 1, 1) + mm(stream, n_cat[h, :, cols(t)], 1, 1)

        @pl.loop(0, tiles // 2)
        def _(i):
            for u in (0, 1):
                arrived(h, prod_copy(h, 2 * i + u))
            one, two = (mixed(2 * i + u, x.at[u]) for u in (0, 1))
            logits[:, :32] += one + two

    sums = logits[...]
    sums = (sums + pltpu.roll(sums, PART - 16, 1))[:, :16]
    lane = lax.broadcasted_iota(jnp.int32, sums.shape, 1)
    hot = lax.broadcasted_iota(jnp.int32, (16, count), 0) == target_ref[...]
    hot = jnp.where(hot, 1.0, 0.0).astype(bf16)
    eye = lax.broadcasted_iota(jnp.int32, (16, 16), 0) == lax.broadcasted_iota(jnp.int32, (16, 16), 1)
    one_hot = mm(hot, jnp.where(eye, 1.0, 0.0).astype(bf16), 0, 0)
    exponent = jnp.where(lane < 4, jnp.exp(sums), 0.0)
    softmax_out = exponent / jnp.sum(exponent, axis=1, keepdims=True)
    grad = loss_scale * (softmax_out - one_hot)
    lg[...] = grad
    for side in (0, 1):
        start(side, lg_copy(side))

    g_high, g_low = split_bf16(grad)
    swap = (lax.broadcasted_iota(jnp.int32, (16, 16), 0) + lax.broadcasted_iota(jnp.int32, (16, 16), 1)) == 3
    swap = jnp.where(swap, 1.0, 0.0).astype(bf16)
    r_high, r_low = mm(g_high, swap).astype(bf16), mm(g_low, swap).astype(bf16)

    @pl.loop(0, tiles)
    def _(t):
        one, two = gated_s[t], gated_s[tiles + t]
        total = (mm(g_high, one, 0, 0) + mm(g_low, one, 0, 0)) + (mm(r_high, two, 0, 0) + mm(r_low, two, 0, 0))
        a_own[:, cols(t)] = total[:8]

    def a_copy(d, slot):
        p = shard_peer(d)
        return send(a_own.at[:, pl.ds(pl.multiple_of(p * own, 128), own)], a_in.at[slot], a_ss.at[d - 1],
                    a_rs.at[slot], (s, p))

    def b_copy(d, slot):
        return send(b_own, b_in.at[slot], b_ss.at[d - 1], b_rs.at[slot], (seq_peer(d), f))

    for d in range(1, shards):
        a_copy(d, f).start()

    spot = lax.broadcasted_iota(jnp.int32, (16, 48), 1)
    lane48 = lax.broadcasted_iota(jnp.int32, (16, 48), 0)
    to_high = jnp.where((spot == lane48) | (spot == lane48 + 16), 1.0, 0.0).astype(bf16)
    to_low = jnp.where(spot == lane48 + 32, 1.0, 0.0).astype(bf16)

    def spread(value):
        high, low = split_bf16(value)
        return (mm(high, to_high) + mm(low, to_low)).astype(bf16)

    local = spread(lg[...])
    coef[0, :count] = local
    coef[1, far:] = local
    for side in (0, 1):
        arrived(side, lg_copy(side))
    coef[0, count:] = spread(lg_high[...])
    coef[1, :far] = spread(lg_low[...])

    def out_copy(m, h, t):
        there = pl.ds(pl.multiple_of(h * half + t * LANES, LANES), LANES)
        return pltpu.make_async_copy(done.at[m, :, there], (qo_ref, ko_ref, vo_ref)[m].at[:, there],
                                     out_sems.at[m, h * tiles + t])

    for h in (0, 1):

        def backward(t, x, grads, pg, feat):
            part = mm(coef[h], m_cat[h, :, cols(t)])
            if h:
                factors = ((0, far, gate_low[:, cols(t)]), (far, count, gate[1, rows - count :, cols(t)]))
            else:
                factors = ((0, count, gate[0, :count, cols(t)]), (count, far, gate_high[:, cols(t)]))
            for at, size, factor in factors:
                x[at : at + size] = (part[at : at + size] * factor.astype(f32)).astype(bf16)
            mine = count + far - rows if h else 0
            feat[0] = part[mine : mine + rows, :] * mix[h * tiles + t]
            banded(1 - h, t, x, pg, 0)
            feat[1] = pg[0] * feat_v[h, :, cols(t)]
            feat[2] = pg[0] * feat_k[h, :, cols(t)]
            there = pl.ds(pl.multiple_of(h * half + t * LANES, LANES), LANES)
            for m in range(3):
                taps = [taps_ref[m, j : j + 1, cols(t)] for j in range(taps_n)]
                size = count + EDGE
                near, away = short_conv(taps, lambda a, n: feat[m, a : a + n, :], EDGE if h else 0, -1 if h else 1, size)
                near = near[EDGE:] if h else near[:count]
                done[m, :, there] = (near + away[4 : 4 + count]).astype(bf16)

        @pl.loop(0, tiles // 2)
        def _(i):
            for u in (0, 1):
                arrived(1 - h, gate_copy(1 - h, 2 * i + u))
            for u in (0, 1):
                backward(2 * i + u, x.at[u], grads, pg.at[u], feat.at[u])
            for u in (0, 1):
                for m in range(3):
                    out_copy(m, h, 2 * i + u).start()

        if h == 0:
            total = a_own[:, pl.ds(pl.multiple_of(f * own, 128), own)]
            for d in range(1, shards):
                a_copy(d, shard_peer(d)).wait_recv()
                total = total + a_in[shard_peer(d)]
            b_own[...] = total
            for d in range(1, seqs):
                b_copy(d, s).start()

    total = b_own[...]
    for d in range(1, seqs):
        b_copy(d, seq_peer(d)).wait_recv()
        total = total + b_in[seq_peer(d)]
    a_ref[...] = total * (1.0 / loss_scale)

    @pl.loop(0, tiles)
    def _(t):
        for h in (0, 1):
            for m in range(3):
                out_copy(m, h, t).wait()

    for side in (0, 1):
        for m in range(3):
            sent(side, rim_copy(side, m))
        sent(side, lg_copy(side))

        @pl.loop(0, tiles)
        def _(t):
            sent(side, prod_copy(side, t))
            sent(side, gate_copy(side, t))

    for d in range(1, shards):
        m_copy(d, f).wait_send()
        a_copy(d, f).wait_send()
    for d in range(1, seqs):
        b_copy(d, s).wait_send()


def finish_kernel(a_ref, head_ref, q_ref, k_ref, v_ref, qo_ref, ko_ref, vo_ref, out_ref, head8):
    @pl.when(pl.program_id(0) == 0)
    def _():
        head8[...] = jnp.zeros_like(head8)
        head8[: head_ref.shape[0]] = head_ref[...]

    for src, dst in ((q_ref, qo_ref), (k_ref, ko_ref), (v_ref, vo_ref)):
        dst[...] = src[...]
    a_high, a_low = split_bf16(a_ref[...])
    h_high, h_low = split_bf16(head8[...])
    out_ref[...] = mm(a_high, h_high, 0, 0) + (mm(a_high, h_low, 0, 0) + mm(a_low, h_high, 0, 0))


def per_device(sizes, query, key, value, stream, targets, short_filter, med_filter, out_weight, head):
    genomes, count, width = query.shape
    half = width // 2
    tiles = half // LANES
    rows = count + 2 * EDGE
    far = count - RIM
    own = out_weight.shape[0]
    taps = short_filter.shape[0]
    seqs, shards = sizes
    assert genomes == 1 and med_filter.shape == (PART, half // 16) and taps <= EDGE and ROWS < rows <= 2 * ROWS
    query, key, value, stream = (a.reshape(count, width) for a in (query, key, value, stream))

    sds = jax.ShapeDtypeStruct
    vmem = pl.BlockSpec(memory_space=pltpu.VMEM)
    hbm = pl.BlockSpec(memory_space=pl.ANY)
    dma = pltpu.SemaphoreType.DMA
    query_grad, key_grad, value_grad, a_sum = pl.pallas_call(
        functools.partial(block_kernel, sizes),
        in_specs=[hbm] * 4 + [vmem] * 3 + [hbm, vmem],
        out_specs=[hbm] * 3 + [vmem],
        out_shape=[sds((count, width), bf16)] * 3 + [sds((8, own), f32)],
        scratch_shapes=[
            pltpu.VMEM((count, width), bf16), pltpu.VMEM((count, width), bf16), pltpu.VMEM((count, width), bf16),
            pltpu.VMEM((count, width), bf16), pltpu.VMEM((own, half), bf16), pltpu.VMEM((3, count, width), bf16),
            pltpu.VMEM((3, RIM, width), bf16), pltpu.VMEM((3, RIM, width), bf16),
            pltpu.VMEM((2, 3, count + 2 * RIM, LANES), f32),
            pltpu.VMEM((2, rows, half), bf16), pltpu.VMEM((2, rows, half), bf16),
            pltpu.VMEM((PART, half), bf16), pltpu.VMEM((PART, half), bf16),
            pltpu.VMEM((far, half), bf16), pltpu.VMEM((far, half), bf16),
            pltpu.VMEM((2, rows, half), f32), pltpu.VMEM((2, rows, half), f32),
            pltpu.VMEM((2 * tiles, rows, LANES), f32),
            pltpu.VMEM((2, half // PART, 8 * ROWS, 2 * PART), bf16),
            pltpu.VMEM((2, count + far, LANES), bf16),
            pltpu.VMEM((2 * tiles, count, LANES), bf16),
            pltpu.VMEM((count, PART), f32), pltpu.VMEM((count, 16), f32),
            pltpu.VMEM((far, 16), f32), pltpu.VMEM((far, 16), f32),
            pltpu.VMEM((8, half), f32), pltpu.VMEM((shards, 8, own), f32), pltpu.VMEM((8, half), f32),
            pltpu.VMEM((2, 48, half), bf16), pltpu.VMEM((2, 32, half), bf16), pltpu.VMEM((2, count + far, 48), bf16),
            pltpu.VMEM((PART, LANES), f32),
            pltpu.VMEM((2, 1, rows, LANES), f32), pltpu.VMEM((2, 3, rows, LANES), f32),
            pltpu.VMEM((8, half), f32), pltpu.VMEM((shards, 8, own), f32), pltpu.VMEM((seqs, 8, own), f32),
            pltpu.VMEM((8, own), f32),
            dma((5,)), dma((3, 2 * tiles)), dma((2, 3)), dma((2, 3)), dma((2, tiles)), dma((2, tiles)), dma((2, tiles)), dma((2, tiles)),
            dma((2,)), dma((2,)), dma((shards,)), dma((shards,)), dma((shards,)), dma((shards,)),
            dma((seqs,)), dma((seqs,)),
        ],
        compiler_params=pltpu.CompilerParams(collective_id=0, has_side_effects=True, vmem_limit_bytes=VMEM_LIMIT),
        cost_estimate=pl.CostEstimate(flops=1024 * count * width * 8, bytes_accessed=20 * count * width, transcendentals=0),
        name="hyena_block",
    )(query, key, value, stream, targets, short_filter.transpose(1, 0, 2), med_filter, out_weight, head)

    steps = own // 128
    piece = pl.BlockSpec((count, width // steps), lambda i: (0, i))
    query_grad, key_grad, value_grad, out_grad = pl.pallas_call(
        finish_kernel,
        grid=(steps,),
        in_specs=[pl.BlockSpec((8, 128), lambda i: (0, i)), pl.BlockSpec((NUC, half), lambda i: (0, 0))] + [piece] * 3,
        out_specs=[piece] * 3 + [pl.BlockSpec((128, half), lambda i: (i, 0))],
        out_shape=[sds((count, width), bf16)] * 3 + [sds((own, half), f32)],
        scratch_shapes=[pltpu.VMEM((8, half), f32)],
        compiler_params=pltpu.CompilerParams(vmem_limit_bytes=VMEM_LIMIT // 2),
        name="finish",
    )(a_sum, head, query_grad, key_grad, value_grad)
    return (query_grad[None], key_grad[None], value_grad[None], out_grad)


def solution(mesh):
    rows = P("fsdp", "seq", None)
    return jax.shard_map(
        functools.partial(per_device, (mesh.shape["seq"], mesh.shape["fsdp"])),
        mesh=mesh,
        in_specs=(rows, rows, rows, rows, P("fsdp", "seq"), P(), P(), P("fsdp", None), P()),
        out_specs=(rows, rows, rows, P("fsdp", None)),
        check_vma=False,
    )
```

time: 187 us -> 74 us (0.40)
  the two profiles are of different devices: /device:TPU:1 before, /device:TPU:4 now
where the time goes in v2:
time: 74 us; the launch traced here: 73.7 us
  Pallas kernels  68.4 us (92%)
  local copies, waits for them, and re-layouts  4.66 us (6%)
    pallas_call x1, Pallas kernels, per_device(): pl.pallas_call(functools.partial(block_kernel, sizes), in_specs=[hbm] * 4...  63.8 us
    unnamed x10, local copies, waits for them, and re-layouts  4.66 us
    pallas_call x1, Pallas kernels, per_device(): pl.pallas_call(finish_kernel, grid=(steps,), in_specs=[pl.BlockSpec((8, 1...  4.53 us

profile of v2, /device:TPU:4, one launch (start us, length us, event | category | flops | bytes accessed | tf_op | source)
XLA Modules:
  0.0 73.7 jit_solution(16278504407490461066)
XLA Ops:
  0.6 0.0 copy-start.3
  0.6 63.8 %hyena_block.1 = (bf16[160,4096]{1,0:T(8,128)(2,1)}, bf16[160,4096]{1,0:T(8,128)(2,1)}, bf16[160,4096]{1,0:T(8,128)(2,1)}, f32[8,512]{1,0:T(8,128)}) custom-call(bf16[160,4096]{1,0:T(8,128)(2,1)} %bitcast.8, bf16[160,4096]{1,0:T(8,128)(2,1)} %bitcast.9, bf16[160,4096]{1,0:T(8,128)(2,1)} %bitcast.10, bf16[160,4096]{1,0:T(8,128)(2,1)} %bitcast.11, ...), custom_call_target="tpu_custom_call" | custom-call | flops 5368709120 | bytes 13107200 | tf_op jit(solution)/shard_map/hyena_block/pallas_call | solution.py:427
  64.5 0.0 copy-done.3
  64.5 0.0 copy-start
  64.5 1.3 %copy-done = bf16[160,4096]{1,0:T(8,128)(2,1)S(1)} copy-done((bf16[160,4096]{1,0:T(8,128)(2,1)S(1)}, bf16[160,4096]{1,0:T(8,128)(2,1)}, u32[]{:S(2)}) %copy-start) | copy-done | bytes 1310744
  65.8 0.0 copy-start.1
  65.8 1.3 %copy-done.1 = bf16[160,4096]{1,0:T(8,128)(2,1)S(1)} copy-done((bf16[160,4096]{1,0:T(8,128)(2,1)S(1)}, bf16[160,4096]{1,0:T(8,128)(2,1)}, u32[]{:S(2)}) %copy-start.1) | copy-done | bytes 1310744
  67.1 0.0 copy-start.2
  67.1 1.3 %copy-done.2 = bf16[160,4096]{1,0:T(8,128)(2,1)S(1)} copy-done((bf16[160,4096]{1,0:T(8,128)(2,1)S(1)}, bf16[160,4096]{1,0:T(8,128)(2,1)}, u32[]{:S(2)}) %copy-start.2) | copy-done | bytes 1310744
  68.4 0.0 copy-start.4
  68.4 0.7 copy-done.4
  69.2 4.5 %finish.1 = (bf16[160,4096]{1,0:T(8,128)(2,1)}, bf16[160,4096]{1,0:T(8,128)(2,1)}, bf16[160,4096]{1,0:T(8,128)(2,1)}, f32[512,2048]{1,0:T(8,128)}) custom-call(f32[8,512]{1,0:T(8,128)S(1)} %copy-done.4, f32[4,2048]{1,0:T(4,128)S(1)} %copy-done.3, bf16[160,4096]{1,0:T(8,128)(2,1)S(1)} %copy-done, bf16[160,4096]{1,0:T(8,128)(2,1)S(1)} %copy-done.1, ...), custom_call_target="tpu_custom_call" | custom-call | tf_op jit(solution)/shard_map/finish/pallas_call | solution.py:464
Async XLA Ops:
  0.6 63.8 %copy-start.3 = (f32[4,2048]{1,0:T(4,128)S(1)}, f32[4,2048]{1,0:T(4,128)}, u32[]{:S(2)}) copy-start(f32[4,2048]{1,0:T(4,128)} %head_ref.3) | copy-start | bytes 98308
  64.5 1.3 %copy-start = (bf16[160,4096]{1,0:T(8,128)(2,1)S(1)}, bf16[160,4096]{1,0:T(8,128)(2,1)}, u32[]{:S(2)}) copy-start(bf16[160,4096]{1,0:T(8,128)(2,1)} %get-tuple-element.13.q_ref) | copy-start | bytes 3932164
  65.8 1.3 %copy-start.1 = (bf16[160,4096]{1,0:T(8,128)(2,1)S(1)}, bf16[160,4096]{1,0:T(8,128)(2,1)}, u32[]{:S(2)}) copy-start(bf16[160,4096]{1,0:T(8,128)(2,1)} %get-tuple-element.14.k_ref) | copy-start | bytes 3932164
  67.1 1.3 %copy-start.2 = (bf16[160,4096]{1,0:T(8,128)(2,1)S(1)}, bf16[160,4096]{1,0:T(8,128)(2,1)}, u32[]{:S(2)}) copy-start(bf16[160,4096]{1,0:T(8,128)(2,1)} %get-tuple-element.15.v_ref) | copy-start | bytes 3932164
  68.4 0.7 copy-start.4

commit v3 on v2

--- a/solution.py
+++ b/solution.py
@@ -29,16 +29,17 @@
     return lax.dot_general(a, b, (((ca,), (cb,)), ((), ())), preferred_element_type=f32)
 
 
-def short_conv(taps, x, first, step, size):
+def short_conv(taps, ref, at, size, later):
+    first, step = (at, 1) if later else (at - EDGE, -1)
     near = far = None
     for j in range(4):
-        moved = x(first + step * j, size)
-        term = taps[j] * moved
+        moved = ref[first + step * j : first + step * j + size + EDGE, :]
+        term = taps[j] * (moved[:size] if later else moved[EDGE:])
         near = term if near is None else near + term
         if j + 4 < len(taps):
             term = taps[j + 4] * moved
             far = term if far is None else far + term
-    return near, far
+    return near + far[4 : 4 + size]
 
 
 def placed(size, reverse, source):
@@ -174,8 +175,10 @@
         def _(i):
             base = grads[pl.ds(pl.multiple_of(i * 8, 8), 8), :]
             for g in range(8):
-                row = jnp.broadcast_to(base[g : g + 1, :], (ROWS, 2 * PART))
-                toep[o, i, g * ROWS : (g + 1) * ROWS, :] = pltpu.roll(row, 0, 1, stride=1, stride_axis=0).astype(bf16)
+                row = jnp.broadcast_to(base[g : g + 1, :], (RIM, 2 * PART))
+                strip = pltpu.roll(row, 0, 1, stride=1, stride_axis=0).astype(bf16)
+                for k in range(0, ROWS, RIM):
+                    toep[o, i, g * ROWS + k : g * ROWS + k + RIM, :] = pltpu.roll(strip, k, 1) if k else strip
 
     def banded(o, t, x, out_ref, slot):
         span = ROWS + PART
@@ -204,26 +207,21 @@
             arrived(side, rim_copy(side, m))
 
     for h in (0, 1):
-        blank = jnp.zeros((EDGE, LANES), f32)
-
         def featured(t, raw):
-            there = pl.ds(pl.multiple_of(h * half + t * LANES, LANES), LANES)
-            feats = []
-            for m, ref in enumerate((q_ref, k_ref, v_ref)):
-                raw[m, :RIM] = rim_low[m, :, there].astype(f32)
-                raw[m, RIM : RIM + count] = ref[:, there].astype(f32)
-                raw[m, RIM + count :] = rim_high[m, :, there].astype(f32)
-                taps = [taps_ref[m, j : j + 1, cols(t)] for j in range(taps_n)]
-                near, away = short_conv(taps, lambda a, n: raw[m, a : a + n, :], EDGE, 1 if h else -1, rows)
-                if h:
-                    value = jnp.concatenate([blank, near[: rows - EDGE] + away[4 : rows - 4]], axis=0)
-                else:
-                    value = jnp.concatenate([near[EDGE:] + away[4 : rows - 4], blank], axis=0)
-                feats.append(value)
-            gate[h, :, cols(t)] = feats[0].astype(bf16)
-            feat_k[h, :, cols(t)] = feats[1]
-            feat_v[h, :, cols(t)] = feats[2]
-            prod[h, :, cols(t)] = (feats[1] * feats[2]).astype(bf16)
+            for part in range(LANES // PART):
+                there = pl.ds(pl.multiple_of(h * half + t * LANES + part * PART, PART), PART)
+                here = pl.ds(pl.multiple_of(t * LANES + part * PART, PART), PART)
+                for m, ref in enumerate((q_ref, k_ref, v_ref)):
+                    raw[m, part, :RIM] = rim_low[m, :, there].astype(f32)
+                    raw[m, part, RIM : RIM + count] = ref[:, there].astype(f32)
+                    raw[m, part, RIM + count :] = rim_high[m, :, there].astype(f32)
+                taps = [[taps_ref[m, j : j + 1, here] for j in range(taps_n)] for m in range(3)]
+                for at, size in ((0, ROWS), (ROWS, rows - ROWS)):
+                    feats = [short_conv(taps[m], raw.at[m, part], at + (0 if h else RIM), size, h == 1) for m in range(3)]
+                    gate[h, at : at + size, here] = feats[0].astype(bf16)
+                    feat_k[h, at : at + size, here] = feats[1]
+                    feat_v[h, at : at + size, here] = feats[2]
+                    prod[h, at : at + size, here] = (feats[1] * feats[2]).astype(bf16)
 
         @pl.loop(0, tiles // 2)
         def _(i):
@@ -335,17 +333,22 @@
             for at, size, factor in factors:
                 x[at : at + size] = (part[at : at + size] * factor.astype(f32)).astype(bf16)
             mine = count + far - rows if h else 0
-            feat[0] = part[mine : mine + rows, :] * mix[h * tiles + t]
+            for c in range(LANES // PART):
+                lanes = slice(c * PART, (c + 1) * PART)
+                feat[0, c] = part[mine : mine + rows, lanes] * mix[h * tiles + t, :, lanes]
             banded(1 - h, t, x, pg, 0)
-            feat[1] = pg[0] * feat_v[h, :, cols(t)]
-            feat[2] = pg[0] * feat_k[h, :, cols(t)]
-            there = pl.ds(pl.multiple_of(h * half + t * LANES, LANES), LANES)
-            for m in range(3):
-                taps = [taps_ref[m, j : j + 1, cols(t)] for j in range(taps_n)]
-                size = count + EDGE
-                near, away = short_conv(taps, lambda a, n: feat[m, a : a + n, :], EDGE if h else 0, -1 if h else 1, size)
-                near = near[EDGE:] if h else near[:count]
-                done[m, :, there] = (near + away[4 : 4 + count]).astype(bf16)
+            for c in range(LANES // PART):
+                lanes = slice(c * PART, (c + 1) * PART)
+                here = pl.ds(pl.multiple_of(t * LANES + c * PART, PART), PART)
+                there = pl.ds(pl.multiple_of(h * half + t * LANES + c * PART, PART), PART)
+                feat[1, c] = pg[0, :, lanes] * feat_v[h, :, here]
+                feat[2, c] = pg[0, :, lanes] * feat_k[h, :, here]
+                size = count // 2
+                for m in range(3):
+                    taps = [taps_ref[m, j : j + 1, here] for j in range(taps_n)]
+                    for at in (0, size):
+                        got = short_conv(taps, feat.at[m, c], at + (RIM if h else 0), size, h == 0)
+                        done[m, at : at + size, there] = got.astype(bf16)
 
         @pl.loop(0, tiles // 2)
         def _(i):
@@ -417,7 +420,7 @@
     own = out_weight.shape[0]
     taps = short_filter.shape[0]
     seqs, shards = sizes
-    assert genomes == 1 and med_filter.shape == (PART, half // 16) and taps <= EDGE and ROWS < rows <= 2 * ROWS
+    assert genomes == 1 and med_filter.shape == (PART, half // 16) and 4 < taps <= EDGE and count % 32 == 0 and ROWS < rows <= 2 * ROWS
     query, key, value, stream = (a.reshape(count, width) for a in (query, key, value, stream))
 
     sds = jax.ShapeDtypeStruct
@@ -433,7 +436,7 @@
             pltpu.VMEM((count, width), bf16), pltpu.VMEM((count, width), bf16), pltpu.VMEM((count, width), bf16),
             pltpu.VMEM((count, width), bf16), pltpu.VMEM((own, half), bf16), pltpu.VMEM((3, count, width), bf16),
             pltpu.VMEM((3, RIM, width), bf16), pltpu.VMEM((3, RIM, width), bf16),
-            pltpu.VMEM((2, 3, count + 2 * RIM, LANES), f32),
+            pltpu.VMEM((2, 3, LANES // PART, count + 2 * RIM, PART), f32),
             pltpu.VMEM((2, rows, half), bf16), pltpu.VMEM((2, rows, half), bf16),
             pltpu.VMEM((PART, half), bf16), pltpu.VMEM((PART, half), bf16),
             pltpu.VMEM((far, half), bf16), pltpu.VMEM((far, half), bf16),
@@ -447,7 +450,7 @@
             pltpu.VMEM((8, half), f32), pltpu.VMEM((shards, 8, own), f32), pltpu.VMEM((8, half), f32),
             pltpu.VMEM((2, 48, half), bf16), pltpu.VMEM((2, 32, half), bf16), pltpu.VMEM((2, count + far, 48), bf16),
             pltpu.VMEM((PART, LANES), f32),
-            pltpu.VMEM((2, 1, rows, LANES), f32), pltpu.VMEM((2, 3, rows, LANES), f32),
+            pltpu.VMEM((2, 1, rows, LANES), f32), pltpu.VMEM((2, 3, LANES // PART, rows, PART), f32),
             pltpu.VMEM((8, half), f32), pltpu.VMEM((shards, 8, own), f32), pltpu.VMEM((seqs, 8, own), f32),
             pltpu.VMEM((8, own), f32),
             dma((5,)), dma((3, 2 * tiles)), dma((2, 3)), dma((2, 3)), dma((2, tiles)), dma((2, tiles)), dma((2, tiles)), dma((2, tiles)),
@@ -468,7 +471,7 @@
         out_specs=[piece] * 3 + [pl.BlockSpec((128, half), lambda i: (i, 0))],
         out_shape=[sds((count, width), bf16)] * 3 + [sds((own, half), f32)],
         scratch_shapes=[pltpu.VMEM((8, half), f32)],
-        compiler_params=pltpu.CompilerParams(vmem_limit_bytes=VMEM_LIMIT // 2),
+        compiler_params=pltpu.CompilerParams(vmem_limit_bytes=VMEM_LIMIT),
         name="finish",
     )(a_sum, head, query_grad, key_grad, value_grad)
     return (query_grad[None], key_grad[None], value_grad[None], out_grad)

time: 74 us -> 68.4 us (0.924)
  the two profiles are of different devices: /device:TPU:4 before, /device:TPU:1 now
where the time goes in v3:
time: 68.4 us; the launch traced here: 67.5 us
  Pallas kernels  66.8 us (98%)
    pallas_call x1, Pallas kernels, per_device(): pl.pallas_call(functools.partial(block_kernel, sizes), in_specs=[hbm] * 4...  60.2 us
    pallas_call x1, Pallas kernels, per_device(): pl.pallas_call(finish_kernel, grid=(steps,), in_specs=[pl.BlockSpec((8, 1...  6.58 us

profile of v3, /device:TPU:1, one launch (start us, length us, event | category | flops | bytes accessed | tf_op | source)
XLA Modules:
  0.0 67.5 jit_solution(16420793623166818787)
XLA Ops:
  0.6 60.2 %hyena_block.1 = (bf16[160,4096]{1,0:T(8,128)(2,1)}, bf16[160,4096]{1,0:T(8,128)(2,1)}, bf16[160,4096]{1,0:T(8,128)(2,1)}, f32[8,512]{1,0:T(8,128)}) custom-call(bf16[160,4096]{1,0:T(8,128)(2,1)} %bitcast.8, bf16[160,4096]{1,0:T(8,128)(2,1)} %bitcast.9, bf16[160,4096]{1,0:T(8,128)(2,1)} %bitcast.10, bf16[160,4096]{1,0:T(8,128)(2,1)} %bitcast.11, ...), custom_call_target="tpu_custom_call" | custom-call | flops 5368709120 | bytes 13107200 | tf_op jit(solution)/shard_map/hyena_block/pallas_call | solution.py:430
  60.9 6.6 %finish.1 = (bf16[160,4096]{1,0:T(8,128)(2,1)}, bf16[160,4096]{1,0:T(8,128)(2,1)}, bf16[160,4096]{1,0:T(8,128)(2,1)}, f32[512,2048]{1,0:T(8,128)}) custom-call(f32[8,512]{1,0:T(8,128)} %get-tuple-element.12.a_ref, f32[4,2048]{1,0:T(4,128)} %head_ref.3, bf16[160,4096]{1,0:T(8,128)(2,1)} %get-tuple-element.13.q_ref, ...), custom_call_target="tpu_custom_call" | custom-call | tf_op jit(solution)/shard_map/finish/pallas_call | solution.py:467

commit v4 on v3

--- a/solution.py
+++ b/solution.py
@@ -54,10 +54,10 @@
     sizes, q_hbm, k_hbm, v_hbm, stream_hbm, target_ref, taps_ref, med_ref, w_hbm, head_ref,
     qo_ref, ko_ref, vo_ref, a_ref,
     q_ref, k_ref, v_ref, stream_ref, w_ref, done,
-    rim_low, rim_high, raw, gate, prod, prod_low, prod_high, gate_low, gate_high, feat_k, feat_v, mix, toep,
+    edges, kv_out, q_low, q_high, kv_low, kv_high, raw, gate, prod, prod_low, prod_high, gate_low, gate_high, feat_k, feat_v, mix, toep,
     x, gated_s, logits, lg, lg_low, lg_high, head8, m_all, m_full, m_cat, n_cat, coef, grads, pg, feat, a_own, a_in,
     b_in, b_own,
-    in_sems, out_sems, rim_ss, rim_rs, prod_ss, prod_rs, gate_ss, gate_rs, lg_ss, lg_rs, m_ss, m_rs, a_ss, a_rs,
+    edge_sems, in_sems, out_sems, rim_ss, rim_rs, prod_ss, prod_rs, gate_ss, gate_rs, lg_ss, lg_rs, m_ss, m_rs, a_ss, a_rs,
     b_ss, b_rs,
 ):
     seqs, shards = sizes
@@ -70,6 +70,12 @@
     taps_n = taps_ref.shape[1]
     own = w_ref.shape[0]
     has_left, has_right = s > 0, s < seqs - 1
+    ends = [
+        pltpu.make_async_copy(src, edges.at[i], edge_sems.at[i])
+        for i, src in enumerate((k_hbm.at[count - RIM :], v_hbm.at[count - RIM :], k_hbm.at[:RIM], v_hbm.at[:RIM]))
+    ]
+    for end in ends:
+        end.start()
     loads = [
         pltpu.make_async_copy(src, dst, in_sems.at[i])
         for i, (src, dst) in enumerate(
@@ -100,10 +106,12 @@
         return pl.ds(pl.multiple_of(t * LANES, LANES), LANES)
 
     def rim_copy(side, m):
-        ref = (q_hbm, k_hbm, v_hbm)[m]
+        ss, rs, to = rim_ss.at[side, m], rim_rs.at[side, m], (right, left)[side]
+        if m:
+            return send(kv_out.at[side], (kv_low, kv_high)[side], ss, rs, to)
         if side == 0:
-            return send(ref.at[count - RIM :], rim_low.at[m], rim_ss.at[side, m], rim_rs.at[side, m], right)
-        return send(ref.at[:RIM], rim_high.at[m], rim_ss.at[side, m], rim_rs.at[side, m], left)
+            return send(q_hbm.at[count - RIM :, :half], q_low, ss, rs, to)
+        return send(q_hbm.at[:RIM, half:], q_high, ss, rs, to)
 
     def prod_copy(side, t):
         if side == 0:
@@ -141,11 +149,17 @@
             for ref in refs:
                 ref[...] = jnp.zeros_like(ref)
 
-    for side in (0, 1):
-        for m in range(3):
+    for end in ends:
+        end.wait()
+    for side, rows_of in ((0, slice(RIM - EDGE, RIM)), (1, slice(0, EDGE))):
+        pair = [edges[2 * side + i].astype(f32)[rows_of] for i in (0, 1)]
+        kv_out[side] = jnp.concatenate(pair, axis=0).astype(bf16)
+    for m in (1, 0):
+        for side in (0, 1):
             start(side, rim_copy(side, m))
-    clear((rim_low, prod_low, gate_low, lg_low), s == 0)
-    clear((rim_high, prod_high, gate_high, lg_high), s == seqs - 1)
+    clear((q_low, kv_low, prod_low, gate_low, lg_low), s == 0)
+    clear((q_high, kv_high, prod_high, gate_high, lg_high), s == seqs - 1)
+    raw[...] = jnp.zeros_like(raw)
 
     head8[...] = jnp.zeros_like(head8)
     head8[: head_ref.shape[0]] = head_ref[...]
@@ -203,7 +217,7 @@
     for load in loads[1:]:
         load.wait()
     for side in (0, 1):
-        for m in range(3):
+        for m in range(2):
             arrived(side, rim_copy(side, m))
 
     for h in (0, 1):
@@ -211,10 +225,17 @@
             for part in range(LANES // PART):
                 there = pl.ds(pl.multiple_of(h * half + t * LANES + part * PART, PART), PART)
                 here = pl.ds(pl.multiple_of(t * LANES + part * PART, PART), PART)
+                end = RIM + count
+                if h:
+                    raw[0, part, end:] = q_high[:, here].astype(f32)
+                else:
+                    raw[0, part, :RIM] = q_low[:, here].astype(f32)
+                low, high = kv_low[:, there].astype(f32), kv_high[:, there].astype(f32)
+                for m in (1, 2):
+                    raw[m, part, RIM - EDGE : RIM] = low[(m - 1) * EDGE : m * EDGE]
+                    raw[m, part, end : end + EDGE] = high[(m - 1) * EDGE : m * EDGE]
                 for m, ref in enumerate((q_ref, k_ref, v_ref)):
-                    raw[m, part, :RIM] = rim_low[m, :, there].astype(f32)
-                    raw[m, part, RIM : RIM + count] = ref[:, there].astype(f32)
-                    raw[m, part, RIM + count :] = rim_high[m, :, there].astype(f32)
+                    raw[m, part, RIM:end] = ref[:, there].astype(f32)
                 taps = [[taps_ref[m, j : j + 1, here] for j in range(taps_n)] for m in range(3)]
                 for at, size in ((0, ROWS), (ROWS, rows - ROWS)):
                     feats = [short_conv(taps[m], raw.at[m, part], at + (0 if h else RIM), size, h == 1) for m in range(3)]
@@ -229,7 +250,6 @@
                 featured(2 * i + u, raw.at[u])
             for u in (0, 1):
                 start(h, prod_copy(h, 2 * i + u))
-                start(1 - h, gate_copy(1 - h, 2 * i + u))
 
     for d in range(1, shards):
         m_copy(d, shard_peer(d)).wait_recv()
@@ -261,6 +281,8 @@
         def _(i):
             for u in (0, 1):
                 arrived(h, prod_copy(h, 2 * i + u))
+            for u in (0, 1):
+                start(h, gate_copy(h, 2 * i + u))
             one, two = (mixed(2 * i + u, x.at[u]) for u in (0, 1))
             logits[:, :32] += one + two
 
@@ -322,7 +344,7 @@
         return pltpu.make_async_copy(done.at[m, :, there], (qo_ref, ko_ref, vo_ref)[m].at[:, there],
                                      out_sems.at[m, h * tiles + t])
 
-    for h in (0, 1):
+    for h in (1, 0):
 
         def backward(t, x, grads, pg, feat):
             part = mm(coef[h], m_cat[h, :, cols(t)])
@@ -360,7 +382,7 @@
                 for m in range(3):
                     out_copy(m, h, 2 * i + u).start()
 
-        if h == 0:
+        if h == 1:
             total = a_own[:, pl.ds(pl.multiple_of(f * own, 128), own)]
             for d in range(1, shards):
                 a_copy(d, shard_peer(d)).wait_recv()
@@ -382,7 +404,7 @@
                 out_copy(m, h, t).wait()
 
     for side in (0, 1):
-        for m in range(3):
+        for m in range(2):
             sent(side, rim_copy(side, m))
         sent(side, lg_copy(side))
 
@@ -435,7 +457,9 @@
         scratch_shapes=[
             pltpu.VMEM((count, width), bf16), pltpu.VMEM((count, width), bf16), pltpu.VMEM((count, width), bf16),
             pltpu.VMEM((count, width), bf16), pltpu.VMEM((own, half), bf16), pltpu.VMEM((3, count, width), bf16),
-            pltpu.VMEM((3, RIM, width), bf16), pltpu.VMEM((3, RIM, width), bf16),
+            pltpu.VMEM((4, RIM, width), bf16), pltpu.VMEM((2, RIM, width), bf16),
+            pltpu.VMEM((RIM, half), bf16), pltpu.VMEM((RIM, half), bf16),
+            pltpu.VMEM((RIM, width), bf16), pltpu.VMEM((RIM, width), bf16),
             pltpu.VMEM((2, 3, LANES // PART, count + 2 * RIM, PART), f32),
             pltpu.VMEM((2, rows, half), bf16), pltpu.VMEM((2, rows, half), bf16),
             pltpu.VMEM((PART, half), bf16), pltpu.VMEM((PART, half), bf16),
@@ -453,7 +477,7 @@
             pltpu.VMEM((2, 1, rows, LANES), f32), pltpu.VMEM((2, 3, LANES // PART, rows, PART), f32),
             pltpu.VMEM((8, half), f32), pltpu.VMEM((shards, 8, own), f32), pltpu.VMEM((seqs, 8, own), f32),
             pltpu.VMEM((8, own), f32),
-            dma((5,)), dma((3, 2 * tiles)), dma((2, 3)), dma((2, 3)), dma((2, tiles)), dma((2, tiles)), dma((2, tiles)), dma((2, tiles)),
+            dma((4,)), dma((5,)), dma((3, 2 * tiles)), dma((2, 2)), dma((2, 2)), dma((2, tiles)), dma((2, tiles)), dma((2, tiles)), dma((2, tiles)),
             dma((2,)), dma((2,)), dma((shards,)), dma((shards,)), dma((shards,)), dma((shards,)),
             dma((seqs,)), dma((seqs,)),
         ],

time: 68.4 us -> 66.1 us (0.966); the launches traced: 67.5 us -> 65.9 us
  Pallas kernels: 66.8 us -> 65.2 us
    pallas_call x1, Pallas kernels: 60.2 us -> 58.6 us  [per_device(): pl.pallas_call(functools.partial(block_kernel, sizes), in_specs=[hbm] * 4...]
where the time goes in v4:
time: 66.1 us; the launch traced here: 65.9 us
  Pallas kernels  65.2 us (99%)
    pallas_call x1, Pallas kernels, per_device(): pl.pallas_call(functools.partial(block_kernel, sizes), in_specs=[hbm] * 4...  58.6 us
    pallas_call x1, Pallas kernels, per_device(): pl.pallas_call(finish_kernel, grid=(steps,), in_specs=[pl.BlockSpec((8, 1...  6.58 us

profile of v4, /device:TPU:1, one launch (start us, length us, event | category | flops | bytes accessed | tf_op | source)
XLA Modules:
  0.0 65.9 jit_solution(8805664356292225740)
XLA Ops:
  0.6 58.6 %hyena_block.1 = (bf16[160,4096]{1,0:T(8,128)(2,1)}, bf16[160,4096]{1,0:T(8,128)(2,1)}, bf16[160,4096]{1,0:T(8,128)(2,1)}, f32[8,512]{1,0:T(8,128)}) custom-call(bf16[160,4096]{1,0:T(8,128)(2,1)} %bitcast.8, bf16[160,4096]{1,0:T(8,128)(2,1)} %bitcast.9, bf16[160,4096]{1,0:T(8,128)(2,1)} %bitcast.10, bf16[160,4096]{1,0:T(8,128)(2,1)} %bitcast.11, ...), custom_call_target="tpu_custom_call" | custom-call | flops 5368709120 | bytes 13107200 | tf_op jit(solution)/shard_map/hyena_block/pallas_call | solution.py:452
  59.3 6.6 %finish.1 = (bf16[160,4096]{1,0:T(8,128)(2,1)}, bf16[160,4096]{1,0:T(8,128)(2,1)}, bf16[160,4096]{1,0:T(8,128)(2,1)}, f32[512,2048]{1,0:T(8,128)}) custom-call(f32[8,512]{1,0:T(8,128)} %get-tuple-element.12.a_ref, f32[4,2048]{1,0:T(4,128)} %head_ref.3, bf16[160,4096]{1,0:T(8,128)(2,1)} %get-tuple-element.13.q_ref, ...), custom_call_target="tpu_custom_call" | custom-call | tf_op jit(solution)/shard_map/finish/pallas_call | solution.py:491
